TPU v7x, 32 devices: a whole 2x2x4 slice. The times are simulated.
32 devices in a mesh: dp: 8 (over z, x), mp: 4 (over y, core).
Axes of the slice: x: 2, y: 2, z: 4, core: 2. Of those that a mesh axis runs over, the one named last changes fastest.
Arguments:
- tokens: bfloat16 [32768, 1024], P('dp', 'mp'), may hold values from -6 to 6
- cotangent: bfloat16 [32768, 1024], P('dp', 'mp'), may hold values from -6 to 6
- lengths: int32 [32], P('dp'), may hold values from 128 to 1024, as said below
- norm_gain: float32 [2, 1024], replicated, may hold values from 0.5 to 1.5
- norm_shift: float32 [2, 1024], replicated, may hold values from -3 to 3
- qkv_weight: bfloat16 [1024, 3072], P(None, 'mp'), may hold values from -0.1875 to 0.1875
- out_weight: bfloat16 [1024, 1024], P('mp'), may hold values from -0.75 to 0.75
- up_weight: bfloat16 [1024, 4096], P(None, 'mp'), may hold values from -0.1875 to 0.1875
- down_weight: bfloat16 [4096, 1024], P('mp'), may hold values from -0.09375 to 0.09375
- qkv_bias: float32 [3072], P('mp'), may hold values from -3 to 3
- up_bias: float32 [4096], P('mp'), may hold values from -3 to 3
- res_bias: float32 [2, 1024], P(None, 'mp'), may hold values from -3 to 3
- in_factor: float32 [2, 1024, 128], P(None, ('dp', 'mp')), may hold values from -0.1875 to 0.1875
- qkv_factor: float32 [128, 3072], P('dp', 'mp'), may hold values from -0.5 to 0.5
- up_factor: float32 [128, 4096], P('dp', 'mp'), may hold values from -0.5 to 0.5
- out_factor: float32 [1024, 128], P('mp', 'dp'), may hold values from -0.75 to 0.75
- down_factor: float32 [4096, 128], P('mp', 'dp'), may hold values from -0.09375 to 0.09375
- res_factor: float32 [2, 128, 1024], P(None, 'dp', 'mp'), may hold values from -0.5 to 0.5
- in_moments: float32 [2, 2, 1024, 128], P(None, None, ('dp', 'mp')), may hold values from -6 to 6, as said below
- qkv_moments: float32 [2, 128, 3072], P(None, 'dp', 'mp'), may hold values from -6 to 6, as said below
- up_moments: float32 [2, 128, 4096], P(None, 'dp', 'mp'), may hold values from -6 to 6, as said below
- out_moments: float32 [2, 1024, 128], P(None, 'mp', 'dp'), may hold values from -6 to 6, as said below
- down_moments: float32 [2, 4096, 128], P(None, 'mp', 'dp'), may hold values from -6 to 6, as said below
- res_moments: float32 [2, 2, 128, 1024], P(None, None, 'dp', 'mp'), may hold values from -6 to 6, as said below
Outputs:
- result: float32 [32768, 1024], P('dp', 'mp')
- grad_tokens: float32 [32768, 1024], P('dp', 'mp')
- in_grad: float32 [2, 1024, 128], P(None, ('dp', 'mp'))
- qkv_grad: float32 [128, 3072], P('dp', 'mp')
- up_grad: float32 [128, 4096], P('dp', 'mp')
- out_grad: float32 [1024, 128], P('mp', 'dp')
- down_grad: float32 [4096, 128], P('mp', 'dp')
- res_grad: float32 [2, 128, 1024], P(None, 'dp', 'mp')
- merged_qkv: float32 [1024, 3072], P(None, 'mp')
- merged_out: float32 [1024, 1024], P('mp')
- merged_up: float32 [1024, 4096], P(None, 'mp')
- merged_down: float32 [4096, 1024], P('mp')
- in_pruned: float32 [2, 2, 1024, 128], P(None, None, ('dp', 'mp'))
- qkv_pruned: float32 [2, 128, 3072], P(None, 'dp', 'mp')
- up_pruned: float32 [2, 128, 4096], P(None, 'dp', 'mp')
- out_pruned: float32 [2, 1024, 128], P(None, 'mp', 'dp')
- down_pruned: float32 [2, 4096, 128], P(None, 'mp', 'dp')
- res_pruned: float32 [2, 2, 128, 1024], P(None, None, 'dp', 'mp')
Inputs may be any that keep to these rules, and one draw needn't show every extreme that they name: `lengths`: one sequence, chosen by the seed, has exactly 1024. `in_moments`: first member normal, second member between 0.5 and 5. `qkv_moments`: first member normal, second member between 0.5 and 5. `up_moments`: first member normal, second member between 0.5 and 5. `out_moments`: first member normal, second member between 0.5 and 5. `down_moments`: first member normal, second member between 0.5 and 5. `res_moments`: first member normal, second member between 0.5 and 5.
All inputs are finite; a program needn't handle non-finite values.
Results may differ from a plain program's by a relative error of at most 0.0095.
The roundings to bfloat16 on the way count: a program that leaves them out, or rounds other values in their place, can miss the bound.
Values may be sent and summed in bfloat16 or wider, within the bound.
No kernel may reach another device: no remote copies, remote signals or barrier semaphores. Data moves between devices by JAX's collectives and lax.ppermute only.
A program may use at most 256 MiB of HBM per device.

v0:
```python
import math

import jax
import jax.numpy as jnp
from jax import lax
from jax.sharding import PartitionSpec as P

HEAD = 64
ROT = 16


HIGHEST = lax.Precision.HIGHEST
first_fix = 1.0 - math.exp(100.0 * math.log(0.9))
second_fix = 1.0 - math.exp(100.0 * math.log(0.999))


def product(left_side, right_side):
    return jnp.dot(left_side, right_side, preferred_element_type=jnp.float32)


def rows_product(left_side, right_side):
    return lax.dot_general(
        left_side, right_side, (((0,), (0,)), ((), ())), preferred_element_type=jnp.float32
    )


def cols_product(left_side, right_side):
    return lax.dot_general(
        left_side, right_side, (((1,), (1,)), ((), ())), preferred_element_type=jnp.float32
    )


def exact_product(left_side, right_side):
    return jnp.dot(left_side, right_side, precision=HIGHEST, preferred_element_type=jnp.float32)


def split_rows(left_low, right_wide):
    upper = right_wide.astype(jnp.bfloat16)
    lower = (right_wide - upper.astype(jnp.float32)).astype(jnp.bfloat16)
    return rows_product(left_low, upper) + rows_product(left_low, lower)


def split_cols(left_wide, right_low):
    upper = left_wide.astype(jnp.bfloat16)
    lower = (left_wide - upper.astype(jnp.float32)).astype(jnp.bfloat16)
    return cols_product(upper, right_low) + cols_product(lower, right_low)


def normalize(values, gain_row, shift_row):
    centred = values - jnp.mean(values, -1, keepdims=True)
    norm_scale = lax.rsqrt(jnp.mean(centred * centred, -1, keepdims=True) + 1e-05)
    unit_rows = centred * norm_scale
    return (unit_rows * gain_row + shift_row, unit_rows, norm_scale)


def normalize_back(grad_rows, unit_rows, norm_scale, gain_row):
    grad_unit = grad_rows * gain_row
    return norm_scale * (
        grad_unit
        - jnp.mean(grad_unit, -1, keepdims=True)
        - unit_rows * jnp.mean(grad_unit * unit_rows, -1, keepdims=True)
    )


def rotary_tables(length):
    half_rot = ROT // 2
    frequency = 10000.0 ** (-jnp.arange(half_rot, dtype=jnp.float32) * 2.0 / ROT)
    angles = jnp.arange(length, dtype=jnp.float32)[:, None] * frequency[None, :]
    return (jnp.cos(angles)[:, None, :], jnp.sin(angles)[:, None, :])


def rotate(values, cosine_table, sine_table):
    half_rot = ROT // 2
    first_part = values[..., :half_rot]
    second_part = values[..., half_rot:ROT]
    return jnp.concatenate(
        [
            first_part * cosine_table - second_part * sine_table,
            second_part * cosine_table + first_part * sine_table,
            values[..., ROT:],
        ],
        -1,
    )


def rotate_back(gradient, cosine_table, sine_table):
    half_rot = ROT // 2
    first_part = gradient[..., :half_rot]
    second_part = gradient[..., half_rot:ROT]
    return jnp.concatenate(
        [
            first_part * cosine_table + second_part * sine_table,
            second_part * cosine_table - first_part * sine_table,
            gradient[..., ROT:],
        ],
        -1,
    )


def masked_scores(queries, key_side, seq_length):
    length = queries.shape[0]
    position = jnp.arange(length)
    allowed = (position[None, :] <= position[:, None]) & (position[None, :] < seq_length)
    scores = jnp.einsum(
        "qhd,khd->hqk", queries, key_side, preferred_element_type=jnp.float32
    ) * HEAD ** (-0.5)
    return jnp.where(allowed[None], scores, -1e30)


def attend(pieces):
    queries, key_side, values, seq_length = pieces
    scores = masked_scores(queries, key_side, seq_length)
    highest = jnp.max(scores, -1, keepdims=True)
    weights = jnp.exp(scores - highest)
    denominator = jnp.sum(weights, -1, keepdims=True)
    context = jnp.einsum(
        "hqk,khd->qhd",
        (weights / denominator).astype(jnp.bfloat16),
        values,
        preferred_element_type=jnp.float32,
    )
    return (context.astype(jnp.bfloat16), (highest + jnp.log(denominator))[..., 0])


def attend_back(pieces):
    queries, key_side, values, seq_length, log_total, grad_context = pieces
    scores = masked_scores(queries, key_side, seq_length)
    probabilities = jnp.exp(scores - log_total[..., None])
    grad_probs = jnp.einsum(
        "qhd,khd->hqk", grad_context, values, preferred_element_type=jnp.float32
    )
    row_terms = jnp.sum(probabilities * grad_probs, -1, keepdims=True)
    grad_scores = (probabilities * (grad_probs - row_terms)).astype(jnp.bfloat16)
    grad_queries = jnp.einsum(
        "hqk,khd->qhd", grad_scores, key_side, preferred_element_type=jnp.float32
    ) * HEAD ** (-0.5)
    grad_keys = jnp.einsum(
        "hqk,qhd->khd", grad_scores, queries, preferred_element_type=jnp.float32
    ) * HEAD ** (-0.5)
    grad_values = jnp.einsum(
        "hqk,qhd->khd",
        probabilities.astype(jnp.bfloat16),
        grad_context,
        preferred_element_type=jnp.float32,
    )
    return (grad_queries, grad_keys, grad_values)


def adam_step(factor, moment, gradient):
    first_moment = 0.9 * moment[0] + 0.1 * gradient
    second_moment = 0.999 * moment[1] + 0.001 * gradient * gradient
    updated = factor - 0.01 * (first_moment / first_fix) / (
        jnp.sqrt(second_moment / second_fix) + 1e-08
    )
    keep_mask = (jnp.abs(moment[0]) >= 0.5).astype(jnp.float32)
    return (updated, jnp.stack([first_moment * keep_mask, second_moment * keep_mask]))


def gelu_slope(hidden):
    return 0.5 * (1.0 + lax.erf(hidden * (1.0 / math.sqrt(2.0)))) + hidden * jnp.exp(
        -0.5 * hidden * hidden
    ) / math.sqrt(2.0 * math.pi)


def per_device(
    tokens,
    cotangent,
    lengths,
    norm_gain,
    norm_shift,
    qkv_weight,
    out_weight,
    up_weight,
    down_weight,
    qkv_bias,
    up_bias,
    res_bias,
    in_factor,
    qkv_factor,
    up_factor,
    out_factor,
    down_factor,
    res_factor,
    in_moments,
    qkv_moments,
    up_moments,
    out_moments,
    down_moments,
    res_moments,
):
    row_count = tokens.shape[0]
    seq_count = lengths.shape[0]
    length = row_count // seq_count
    heads_here = qkv_weight.shape[1] // (3 * HEAD)
    position = jnp.arange(length)
    valid = (position[None, :] < lengths[:, None]).reshape(row_count, 1)
    inputs_full, cotangent_full = (
        lax.all_gather(tokens, "mp", axis=1, tiled=True),
        lax.all_gather(cotangent, "mp", axis=1, tiled=True),
    )
    upstream = jnp.where(valid, cotangent_full, jnp.zeros_like(cotangent_full))
    own_upstream = jnp.where(valid, cotangent, jnp.zeros_like(cotangent))
    inputs_wide = inputs_full.astype(jnp.float32)
    norm_one, unit_one, scale_one = normalize(inputs_wide, norm_gain[0], norm_shift[0])
    norm_two, unit_two, scale_two = normalize(inputs_wide, norm_gain[1], norm_shift[1])
    first_low = norm_one.astype(jnp.bfloat16)
    second_low = norm_two.astype(jnp.bfloat16)
    in_full = lax.all_gather(in_factor.astype(jnp.bfloat16), ("dp", "mp"), axis=1, tiled=True)
    qkv_cols, up_cols, out_rows, down_rows, res_cols = (
        lax.all_gather(qkv_factor.astype(jnp.bfloat16), "dp", axis=0, tiled=True),
        lax.all_gather(up_factor.astype(jnp.bfloat16), "dp", axis=0, tiled=True),
        lax.all_gather(out_factor.astype(jnp.bfloat16), "dp", axis=1, tiled=True),
        lax.all_gather(down_factor.astype(jnp.bfloat16), "dp", axis=1, tiled=True),
        lax.all_gather(res_factor.astype(jnp.bfloat16), "dp", axis=1, tiled=True),
    )
    qkv_rank = product(first_low, in_full[0]).astype(jnp.bfloat16)
    mixed_rows = product(first_low, qkv_weight) + product(qkv_rank, qkv_cols) + qkv_bias
    mixed_rows = mixed_rows.reshape(seq_count, length, heads_here, 3, HEAD)
    cosine_table, sine_table = rotary_tables(length)
    queries = rotate(mixed_rows[..., 0, :], cosine_table, sine_table).astype(jnp.bfloat16)
    key_side = rotate(mixed_rows[..., 1, :], cosine_table, sine_table).astype(jnp.bfloat16)
    values = mixed_rows[..., 2, :].astype(jnp.bfloat16)
    context, log_total = lax.map(attend, (queries, key_side, values, lengths))
    context_flat = context.reshape(row_count, heads_here * HEAD)
    up_rank = product(second_low, in_full[1]).astype(jnp.bfloat16)
    hidden = product(second_low, up_weight) + product(up_rank, up_cols) + up_bias
    active = jax.nn.gelu(hidden, approximate=False).astype(jnp.bfloat16)
    out_code, down_code = lax.psum(
        (product(context_flat, out_rows), product(active, down_rows)), "mp"
    )
    out_rank = out_code.astype(jnp.bfloat16)
    down_rank = down_code.astype(jnp.bfloat16)
    branch = lax.psum_scatter(
        product(context_flat, out_weight) + product(active, down_weight),
        "mp",
        scatter_dimension=1,
        tiled=True,
    )
    result = (
        tokens.astype(jnp.float32)
        + branch
        + product(out_rank, res_cols[0])
        + product(down_rank, res_cols[1])
        + res_bias[0]
        + res_bias[1]
    )
    result = jnp.where(valid, result, 0.0)
    grad_out_code, grad_down_code = lax.psum(
        (cols_product(own_upstream, res_cols[0]), cols_product(own_upstream, res_cols[1])), "mp"
    )
    grad_out_rank = grad_out_code.astype(jnp.bfloat16)
    grad_down_rank = grad_down_code.astype(jnp.bfloat16)
    grad_res_out = rows_product(out_rank, own_upstream)
    grad_res_down = rows_product(down_rank, own_upstream)
    grad_out_factor = rows_product(context_flat, grad_out_rank)
    grad_down_factor = rows_product(active, grad_down_rank)
    grad_active = cols_product(upstream, down_weight) + cols_product(grad_down_rank, down_rows)
    grad_hidden = (grad_active * gelu_slope(hidden)).astype(jnp.bfloat16)
    grad_up_rank = cols_product(grad_hidden, up_cols)
    grad_up_factor = rows_product(up_rank, grad_hidden)
    grad_in_up = split_rows(second_low, grad_up_rank)
    grad_norm_two = cols_product(grad_hidden, up_weight) + split_cols(grad_up_rank, in_full[1])
    mlp_part = normalize_back(grad_norm_two, unit_two, scale_two, norm_gain[1])
    grad_context = (
        cols_product(upstream, out_weight) + cols_product(grad_out_rank, out_rows)
    ).astype(jnp.bfloat16)
    grad_context = grad_context.reshape(seq_count, length, heads_here, HEAD)
    grad_queries, grad_keys, grad_values = lax.map(
        attend_back, (queries, key_side, values, lengths, log_total, grad_context)
    )
    grad_queries = rotate_back(grad_queries, cosine_table, sine_table)
    grad_keys = rotate_back(grad_keys, cosine_table, sine_table)
    grad_mixed = jnp.stack([grad_queries, grad_keys, grad_values], axis=3)
    grad_mixed = grad_mixed.reshape(row_count, heads_here * 3 * HEAD).astype(jnp.bfloat16)
    grad_qkv_rank = cols_product(grad_mixed, qkv_cols)
    grad_qkv_factor = rows_product(qkv_rank, grad_mixed)
    grad_in_qkv = split_rows(first_low, grad_qkv_rank)
    grad_norm_one = cols_product(grad_mixed, qkv_weight) + split_cols(grad_qkv_rank, in_full[0])
    attn_part = normalize_back(grad_norm_one, unit_one, scale_one, norm_gain[0])
    grad_tokens = lax.psum_scatter(
        mlp_part + attn_part, "mp", scatter_dimension=1, tiled=True
    ) + own_upstream.astype(jnp.float32)
    in_grad = lax.psum_scatter(
        jnp.stack([grad_in_qkv, grad_in_up]), ("dp", "mp"), scatter_dimension=1, tiled=True
    )
    qkv_owned, up_owned, out_owned, down_owned, res_grad = (
        lax.psum_scatter(grad_qkv_factor, "dp", scatter_dimension=0, tiled=True),
        lax.psum_scatter(grad_up_factor, "dp", scatter_dimension=0, tiled=True),
        lax.psum_scatter(grad_out_factor, "dp", scatter_dimension=1, tiled=True),
        lax.psum_scatter(grad_down_factor, "dp", scatter_dimension=1, tiled=True),
        lax.psum_scatter(
            jnp.stack([grad_res_out, grad_res_down]), "dp", scatter_dimension=1, tiled=True
        ),
    )
    new_in, in_pruned = adam_step(in_factor, in_moments, in_grad)
    new_qkv, qkv_pruned = adam_step(qkv_factor, qkv_moments, qkv_owned)
    new_up, up_pruned = adam_step(up_factor, up_moments, up_owned)
    new_out, out_pruned = adam_step(out_factor, out_moments, out_owned)
    new_down, down_pruned = adam_step(down_factor, down_moments, down_owned)
    new_res, res_pruned = adam_step(res_factor, res_moments, res_grad)
    in_whole = lax.all_gather(new_in, ("dp", "mp"), axis=1, tiled=True)
    qkv_whole, up_whole, out_whole, down_whole, res_part = (
        lax.all_gather(new_qkv, "dp", axis=0, tiled=True),
        lax.all_gather(new_up, "dp", axis=0, tiled=True),
        lax.all_gather(new_out, "dp", axis=1, tiled=True),
        lax.all_gather(new_down, "dp", axis=1, tiled=True),
        lax.all_gather(new_res, "dp", axis=1, tiled=True),
    )
    res_whole = lax.all_gather(res_part, "mp", axis=2, tiled=True)
    merged_qkv = qkv_weight.astype(jnp.float32) + exact_product(in_whole[0], qkv_whole)
    merged_out = out_weight.astype(jnp.float32) + exact_product(out_whole, res_whole[0])
    merged_up = up_weight.astype(jnp.float32) + exact_product(in_whole[1], up_whole)
    merged_down = down_weight.astype(jnp.float32) + exact_product(down_whole, res_whole[1])
    return (
        result,
        grad_tokens,
        in_grad,
        qkv_owned,
        up_owned,
        out_owned,
        down_owned,
        res_grad,
        merged_qkv,
        merged_out,
        merged_up,
        merged_down,
        in_pruned,
        qkv_pruned,
        up_pruned,
        out_pruned,
        down_pruned,
        res_pruned,
    )


def solution(mesh):
    placed = (
        P("dp", "mp"),
        P("dp", "mp"),
        P("dp"),
        P(),
        P(),
        P(None, "mp"),
        P("mp", None),
        P(None, "mp"),
        P("mp", None),
        P("mp"),
        P("mp"),
        P(None, "mp"),
        P(None, ("dp", "mp"), None),
        P("dp", "mp"),
        P("dp", "mp"),
        P("mp", "dp"),
        P("mp", "dp"),
        P(None, "dp", "mp"),
        P(None, None, ("dp", "mp"), None),
        P(None, "dp", "mp"),
        P(None, "dp", "mp"),
        P(None, "mp", "dp"),
        P(None, "mp", "dp"),
        P(None, None, "dp", "mp"),
    )
    return jax.shard_map(
        per_device,
        mesh=mesh,
        in_specs=placed,
        out_specs=(
            P("dp", "mp"),
            P("dp", "mp"),
            P(None, ("dp", "mp"), None),
            P("dp", "mp"),
            P("dp", "mp"),
            P("mp", "dp"),
            P("mp", "dp"),
            P(None, "dp", "mp"),
            P(None, "mp"),
            P("mp", None),
            P(None, "mp"),
            P("mp", None),
            P(None, None, ("dp", "mp"), None),
            P(None, "dp", "mp"),
            P(None, "dp", "mp"),
            P(None, "mp", "dp"),
            P(None, "mp", "dp"),
            P(None, None, "dp", "mp"),
        ),
        check_vma=False,
    )
```

profile of v0, /device:TPU:0, one launch (start us, length us, event | category | flops | bytes accessed | tf_op | source)
XLA Modules:
  0.0 1632.0 jit_solution(2677092315197194974)
XLA Ops:
  10.4 32.3 %all_gather.50 = bf16[2,128,256]{2,1,0:T(8,128)(2,1)S(1)} all-gather(bf16[2,16,256]{2,1,0:T(8,128)(2,1)S(1)} %convert_element_type.140), channel_id=1, replica_groups=mesh['dp'=8,'mp'=4] {'dp'}, dimensions={1}, use_global_device_ids=true | all-gather | bytes 147456 | tf_op jit(solution)/shard_map/all_gather | solution.py:214
  50.1 32.4 %all_gather.49 = bf16[256,128]{0,1:T(8,128)(2,1)} all-gather(bf16[256,16]{0,1:T(8,128)(2,1)S(1)} %convert_element_type.138), channel_id=1, replica_groups=mesh['dp'=8,'mp'=4] {'dp'}, dimensions={1}, use_global_device_ids=true | all-gather | bytes 73728 | tf_op jit(solution)/shard_map/all_gather | solution.py:212
  82.8 30.8 %all_gather.47 = bf16[128,768]{1,0:T(8,128)(2,1)S(1)} all-gather(bf16[16,768]{1,0:T(8,128)(2,1)S(1)} %convert_element_type.132), channel_id=1, replica_groups=mesh['dp'=8,'mp'=4] {'dp'}, dimensions={0}, use_global_device_ids=true | all-gather | bytes 221184 | tf_op jit(solution)/shard_map/all_gather | solution.py:210
  113.5 32.8 %all_gather.51 = bf16[1024,128]{0,1:T(8,128)(2,1)} all-gather(bf16[1024,16]{0,1:T(8,128)(2,1)S(1)} %convert_element_type.141), channel_id=1, replica_groups=mesh['dp'=8,'mp'=4] {'dp'}, dimensions={1}, use_global_device_ids=true | all-gather | bytes 294912 | tf_op jit(solution)/shard_map/all_gather | solution.py:213
  146.3 32.7 %all_gather.48 = bf16[128,1024]{1,0:T(8,128)(2,1)} all-gather(bf16[16,1024]{1,0:T(8,128)(2,1)S(1)} %convert_element_type.136), channel_id=1, replica_groups=mesh['dp'=8,'mp'=4] {'dp'}, dimensions={0}, use_global_device_ids=true | all-gather | bytes 294912 | tf_op jit(solution)/shard_map/all_gather | solution.py:211
  179.0 42.9 %all_gather.46 = bf16[2,1024,128]{2,1,0:T(8,128)(2,1)S(1)} all-gather(bf16[2,32,128]{2,1,0:T(8,128)(2,1)S(1)} %convert_element_type.130), channel_id=1, replica_groups=mesh['dp'=8,'mp'=4] {'dp','mp'}, dimensions={1}, use_global_device_ids=true | all-gather | bytes 540672 | tf_op jit(solution)/shard_map/all_gather | solution.py:208
  230.7 6.5 fusion.60
  240.6 7.0 fusion.143
  247.7 6.4 add_add_fusion.1
  254.0 12.6 copy.60
  266.7 16.0 reshape.272
  287.4 8.7 slice_bitcast_fusion
  308.9 67.5 %while.26 = (s32[]{:T(128)}, bf16[4,1024,4,64]{1,3,2,0:T(8,128)(2,1)}, f32[4,4,1024]{2,1,0:T(4,128)}, bf16[4,1024,4,64]{1,3,2,0:T(8,128)(2,1)}, s32[4]{0:T(128)S...) while((s32[]{:T(128)}, bf16[4,1024,4,64]{1,3,2,0:T(8,128)(2,1)}, ...), condition=%wide.region_5.6_spmd, body=%wide.region_2.0_spmd.sunk | while | flops 1126429696 | bytes 56758384 | solution.py:223
  318.6 6.7 fusion.232
  335.4 6.7 fusion.232
  352.2 6.7 fusion.232
  369.0 6.7 fusion.232
  384.8 11.7 fusion.144
  396.5 41.8 %fusion.72 = (bf16[4096,1024]{1,0:T(8,128)(2,1)S(1)}, f32[4096,1024]{1,0:T(8,128)}) fusion(f32[1024]{0:T(1024)S(1)} %copy-done.87, f32[4096,1024]{1,0:T(8,128)} %fusion.144, bf16[4096,128]{1,0:T(8,128)(2,1)S(1)} %copy-done.26, bf16[128,1024]{1,0:T(8,128)(2,1)S(1)} %copy-done.38), kind=kOutput, calls=%fused_computation.86 | convolution fusion | flops 1354760192 | bytes 43257856 | tf_op jit(solution)/shard_map/dot_general | solution.py:18
  445.5 145.9 %all-reduce.2 = (bf16[4096,128]{1,0:T(8,128)(2,1)}, bf16[4096,128]{1,0:T(8,128)(2,1)}, bf16[4096,128]{1,0:T(8,128)(2,1)S(1)}, bf16[4096,128]{1,0:T(8,128)(2,1)}) all-reduce(f32[4096,128]{1,0:T(8,128)S(1)} %copy-done.16, f32[4096,128]{1,0:T(8,128)} %fusion.147, f32[4096,128]{1,0:T(8,128)} %fusion.111, ...), channel_id=1, replica_groups=mesh['dp'=8,'mp'=4] {'mp'}, use_global_device_ids=true, to_apply=%region_7.8 | all-reduce | flops 2097152 | bytes 12582912 | tf_op jit(solution)/shard_map/psum | solution.py:228
  591.5 6.5 fusion.90
  607.6 203.1 %while.27 = (s32[]{:T(128)}, f32[4,1024,4,64]{1,3,2,0:T(8,128)}, f32[4,1024,4,64]{1,3,2,0:T(8,128)}, bf16[4,1024,4,64]{1,3,2,0:T(8,128)(2,1)}, bf16[4,1024,4,64]...) while((s32[]{:T(128)}, f32[4,1024,4,64]{1,3,2,0:T(8,128)}, ...), condition=%wide.region_15.16_spmd, body=%wide.region_13.15_spmd.sunk | while | flops 2724721664 | bytes 185162992 | solution.py:268
  611.1 9.3 fusion.241
  620.3 12.5 multiply_reduce_fusion.2
  632.9 10.3 multiply_convert_fusion.2
  647.7 7.3 fusion.244
  661.7 9.3 fusion.241
  671.0 12.5 multiply_reduce_fusion.2
  683.5 10.3 multiply_convert_fusion.2
  698.3 7.3 fusion.244
  712.3 9.3 fusion.241
  721.6 12.5 multiply_reduce_fusion.2
  734.1 10.3 multiply_convert_fusion.2
  748.9 7.3 fusion.244
  762.9 9.3 fusion.241
  772.2 12.5 multiply_reduce_fusion.2
  784.7 10.3 multiply_convert_fusion.2
  799.5 7.3 fusion.244
  813.0 7.1 copy.74
  828.0 15.6 fusion.91
  843.7 14.8 fusion.78
  873.0 10.6 copy.82
  883.6 7.1 copy.101
  902.1 6.1 fusion.152
  921.7 32.7 %all_gather.56 = f32[2,128,256]{2,1,0:T(8,128)} all-gather(f32[2,16,256]{2,1,0:T(8,128)S(1)} %get-tuple-element.221), channel_id=1, replica_groups=mesh['dp'=8,'mp'=4] {'dp'}, dimensions={1}, use_global_device_ids=true | all-gather | bytes 294912 | tf_op jit(solution)/shard_map/all_gather | solution.py:307
  954.5 77.0 %reduce-scatter.13.cloned.1.call-done = f32[2,32,128]{2,1,0:T(8,128)} async-done(((f32[2,1024,128]{2,1,0:T(8,128)}), f32[2,32,128]{2,1,0:T(8,128)}) %reduce-scatter.13.cloned.1.call-update) | async-done | bytes 32784 | tf_op jit(solution)/shard_map/reduce_scatter | solution.py:283
  1034.4 16.7 %fusion.145 = f32[4096,1024]{1,0:T(8,128)} fusion(bf16[4096,1024]{1,0:T(8,128)(2,1)} %copy-done.17, bf16[1024,1024]{1,0:T(8,128)(2,1)} %param.36), kind=kOutput, calls=%fused_computation.267 | convolution fusion | flops 8589934592 | bytes 27262976 | tf_op jit(solution)/shard_map/dot_general | solution.py:18
  1051.1 14.1 convolution_add_fusion
  1066.3 8.1 fusion.105
  1074.4 8.2 fusion.106
  1082.6 10.5 fusion.150
  1093.2 18.2 %add_multiply_fusion = f32[4096,1024]{1,0:T(8,128)} fusion(f32[4096,1024]{1,0:T(8,128)} %fusion.150, f32[4096,1024]{1,0:T(8,128)} %fusion.105, f32[1024]{0:T(1024)S(1)} %bitcast.379, bf16[2,1024,128]{2,1,0:T(8,128)(2,1)S(1)} %copy-done.23, f32[4096,128]{1,0:T(8,128)S(1)} %fusion.151), kind=kOutput, calls=%fused_computation.93 | convolution fusion | flops 1088421888 | bytes 52695040 | tf_op jit(solution)/shard_map/dot_general | solution.py:28
  1111.4 16.4 %fusion.148 = f32[4096,1024]{1,0:T(8,128)} fusion(bf16[4096,1024]{1,0:T(8,128)(2,1)} %copy-done.2, bf16[1024,1024]{1,0:T(8,128)(2,1)} %param.35), kind=kOutput, calls=%fused_computation.270 | convolution fusion | flops 8589934592 | bytes 27262976 | tf_op jit(solution)/shard_map/dot_general | solution.py:28
  1127.8 26.7 %fusion.132 = (f32[4096]{0:T(1024)S(1)}, f32[4096]{0:T(1024)S(1)}, f32[4096]{0:T(1024)S(1)}, f32[4096]{0:T(1024)S(1)}, f32[4096,1024]{1,0:T(8,128)}) fusion(f32[4096]{0:T(1024)S(1)} %copy-done.60, f32[4096]{0:T(1024)S(1)} %copy-done.48, bf16[4096,1024]{1,0:T(8,128)(2,1)} %all-gather.5.cloned.1.call-done, f32[4096,1024]{1,0:T(8,128)} %add_multiply_fusion, ...), kind=kOutput, calls=%fused_computation.260 | convolution fusion | flops 1126154240 | bytes 77959168 | tf_op jit(solution)/shard_map/dot_general | solution.py:28
  1154.5 21.1 %fusion.66 = f32[4096,1024]{1,0:T(8,128)} fusion(bf16[4096,1024]{1,0:T(8,128)(2,1)} %all-gather.5.cloned.1.call-done, f32[4096,1024]{1,0:T(8,128)} %add_multiply_fusion, f32[4096,1024]{1,0:T(8,128)} %get-tuple-element.240, f32[4096]{0:T(1024)S(1)} %broadcast_multiply_fusion, f32[4096]{0:T(1024)S(1)} %broadcast_multiply_fusion.1, ...), kind=kLoop, calls=%fused_computation.80 | loop fusion | flops 46137344 | bytes 58818560 | tf_op jit(solution)/shard_map/add | solution.py:281
  1178.1 32.2 %all_gather.55 = f32[256,128]{0,1:T(8,128)} all-gather(f32[256,16]{0,1:T(8,128)S(1)} %get-tuple-element.229), channel_id=1, replica_groups=mesh['dp'=8,'mp'=4] {'dp'}, dimensions={1}, use_global_device_ids=true | all-gather | bytes 147456 | tf_op jit(solution)/shard_map/all_gather | solution.py:305
  1213.9 31.4 %all_gather.54 = f32[128,768]{1,0:T(8,128)S(1)} all-gather(f32[16,768]{1,0:T(8,128)S(1)} %get-tuple-element.219), channel_id=1, replica_groups=mesh['dp'=8,'mp'=4] {'dp'}, dimensions={0}, use_global_device_ids=true | all-gather | bytes 442368 | tf_op jit(solution)/shard_map/all_gather | solution.py:303
  1247.7 41.7 %reduce-scatter.21.cloned.1.call-done = f32[1024,16]{0,1:T(8,128)} async-done(((f32[1024,128]{0,1:T(8,128)}), f32[1024,16]{0,1:T(8,128)}) %reduce-scatter.21.cloned.1.call-update) | async-done | bytes 65552 | tf_op jit(solution)/shard_map/reduce_scatter | solution.py:290
  1291.8 31.5 %all_gather.58 = f32[128,1024]{1,0:T(8,128)S(1)} all-gather(f32[16,1024]{1,0:T(8,128)S(1)} %get-tuple-element.217), channel_id=1, replica_groups=mesh['dp'=8,'mp'=4] {'dp'}, dimensions={0}, use_global_device_ids=true | all-gather | bytes 589824 | tf_op jit(solution)/shard_map/all_gather | solution.py:304
  1323.3 31.7 %all_gather.59 = f32[1024,128]{0,1:T(8,128)S(1)} all-gather(f32[1024,16]{0,1:T(8,128)S(1)} %get-tuple-element.215), channel_id=1, replica_groups=mesh['dp'=8,'mp'=4] {'dp'}, dimensions={1}, use_global_device_ids=true | all-gather | bytes 589824 | tf_op jit(solution)/shard_map/all_gather | solution.py:306
  1359.6 6.1 convert_add_fusion
  1371.7 6.5 convert_add_fusion.1
  1378.2 114.2 %reduce-scatter.9.cloned.1.call-done = f32[4096,256]{1,0:T(8,128)} async-done(((f32[4096,1024]{1,0:T(8,128)}), f32[4096,256]{1,0:T(8,128)}) %reduce-scatter.9.cloned.1.call-update) | async-done | bytes 4194320 | tf_op jit(solution)/shard_map/reduce_scatter | solution.py:233
  1500.1 120.9 %reduce-scatter.11.cloned.1.call-done = f32[4096,256]{1,0:T(8,128)} async-done(((f32[4096,1024]{1,0:T(8,128)}), f32[4096,256]{1,0:T(8,128)}) %reduce-scatter.11.cloned.1.call-update) | async-done | bytes 4194320 | tf_op jit(solution)/shard_map/reduce_scatter | solution.py:280
  (391 shorter events, 236.5 us)
Async XLA Ops:
  7.2 39.3 %copy-start.10 = (bf16[4096,256]{1,0:T(8,128)(2,1)S(1)}, bf16[4096,256]{1,0:T(8,128)(2,1)}, u32[]{:S(2)}) copy-start(bf16[4096,256]{1,0:T(8,128)(2,1)} %param.29) | copy-start | bytes 6291460
  7.2 42.8 %copy-start.74 = (f32[256,16]{0,1:T(8,128)S(1)}, f32[256,16]{0,1:T(8,128)}, u32[]{:S(2)}) copy-start(f32[256,16]{0,1:T(8,128)} %param.43) | copy-start | bytes 49156
  7.2 42.8 %copy-start.81 = (f32[2,1024]{1,0:T(2,128)S(1)}, f32[2,1024]{1,0:T(2,128)}, u32[]{:S(2)}) copy-start(f32[2,1024]{1,0:T(2,128)} %param.31) | copy-start | bytes 24580
  7.2 42.8 %copy-start.82 = (f32[2,1024]{1,0:T(2,128)S(1)}, f32[2,1024]{1,0:T(2,128)}, u32[]{:S(2)}) copy-start(f32[2,1024]{1,0:T(2,128)} %param.32) | copy-start | bytes 24580
  7.2 42.8 %copy-start.67 = (f32[2,32,128]{2,1,0:T(8,128)S(1)}, f32[2,32,128]{2,1,0:T(8,128)}, u32[]{:S(2)}) copy-start(f32[2,32,128]{2,1,0:T(8,128)} %param.40) | copy-start | bytes 98308
  7.2 42.8 %copy-start.62 = (f32[16,768]{1,0:T(8,128)S(1)}, f32[16,768]{1,0:T(8,128)}, u32[]{:S(2)}) copy-start(f32[16,768]{1,0:T(8,128)} %param.41) | copy-start | bytes 147460
  7.3 42.8 %copy-start.55 = (f32[16,1024]{1,0:T(8,128)S(1)}, f32[16,1024]{1,0:T(8,128)}, u32[]{:S(2)}) copy-start(f32[16,1024]{1,0:T(8,128)} %param.42) | copy-start | bytes 196612
  7.3 42.9 %copy-start.57 = (f32[1024,16]{0,1:T(8,128)S(1)}, f32[1024,16]{0,1:T(8,128)}, u32[]{:S(2)}) copy-start(f32[1024,16]{0,1:T(8,128)} %param.44) | copy-start | bytes 196612
  7.3 214.7 %all-gather.5.cloned.1.call-start = ((), (), s32[]{:S(2)}) async-start(), calls=%async_computation.8 | async-start | bytes 10485760 | tf_op jit(solution)/shard_map/all_gather | solution.py:198
  8.0 583.5 %all-gather.7.cloned.1.call-start = ((), (), s32[]{:S(2)}) async-start(), calls=%async_computation.10 | async-start | bytes 10485760 | tf_op jit(solution)/shard_map/all_gather | solution.py:199
  8.8 911.3 %reduce-scatter.23.cloned.1.call-start = ((), (), s32[]{:S(2)}) async-start(), calls=%async_computation.17 | async-start | bytes 294912 | tf_op jit(solution)/shard_map/reduce_scatter | solution.py:291
  9.6 36.9 %copy-start.69 = (pred[1,8,4,128]{3,1,2,0:T(8,128)(4,1)}, pred[1,8,4,128]{3,1,2,0:T(8,128)(4,1)S(1)}, u32[]{:S(2)}) copy-start(pred[1,8,4,128]{3,1,2,0:T(8,128)(4,1)S(1)} %copy.103) | copy-start | bytes 12292
  50.0 180.7 %copy-start.76 = (f32[1,1024]{1,0:T(1,128)}, f32[1,1024]{1,0:T(1,128)S(1)}, u32[]{:S(2)}) copy-start(f32[1,1024]{1,0:T(1,128)S(1)} %get-tuple-element.230) | copy-start | bytes 12292
  50.0 180.7 %copy-start.78 = (f32[1,1024]{1,0:T(1,128)}, f32[1,1024]{1,0:T(1,128)S(1)}, u32[]{:S(2)}) copy-start(f32[1,1024]{1,0:T(1,128)S(1)} %get-tuple-element.231) | copy-start | bytes 12292
  82.7 220.1 %copy-start.49 = (f32[1024,8]{0,1:T(8,128)}, f32[1024,8]{0,1:T(8,128)S(1)}, u32[]{:S(2)}) copy-start(f32[1024,8]{0,1:T(8,128)S(1)} %get-tuple-element.236) | copy-start | bytes 98308
  82.8 220.1 %copy-start.51 = (f32[1024,8]{0,1:T(8,128)}, f32[1024,8]{0,1:T(8,128)S(1)}, u32[]{:S(2)}) copy-start(f32[1024,8]{0,1:T(8,128)S(1)} %get-tuple-element.237) | copy-start | bytes 98308
  113.5 134.1 %copy-start.32 = (bf16[128,768]{1,0:T(8,128)(2,1)}, bf16[128,768]{1,0:T(8,128)(2,1)S(1)}, u32[]{:S(2)}) copy-start(bf16[128,768]{1,0:T(8,128)(2,1)S(1)} %all_gather.47) | copy-start | bytes 589828
  221.9 74.1 %copy-start.22 = (bf16[2,1024,128]{2,1,0:T(8,128)(2,1)}, bf16[2,1024,128]{2,1,0:T(8,128)(2,1)S(1)}, u32[]{:S(2)}) copy-start(bf16[2,1024,128]{2,1,0:T(8,128)(2,1)S(1)} %all_gather.46) | copy-start | bytes 1572868
  282.7 13.4 slice-start.2
  376.4 20.0 %copy-start.13 = (bf16[4,1024,4,64]{1,3,2,0:T(8,128)(2,1)}, bf16[4,1024,4,64]{1,3,2,0:T(8,128)(2,1)S(1)}, u32[]{:S(2)}) copy-start(bf16[4,1024,4,64]{1,3,2,0:T(8,128)(2,1)S(1)} %get-tuple-element.431) | copy-start | bytes 6291460
  384.7 11.7 copy-start.26
  384.7 11.7 copy-start.38
  384.7 11.7 copy-start.87
  396.5 45.4 %copy-start.40 = (bf16[1024,128]{0,1:T(8,128)(2,1)S(1)}, bf16[1024,128]{0,1:T(8,128)(2,1)}, u32[]{:S(2)}) copy-start(bf16[1024,128]{0,1:T(8,128)(2,1)} %all_gather.51) | copy-start | bytes 786436
  441.8 149.7 %copy-start.70 = (pred[1,8,4,128]{3,1,2,0:T(8,128)(4,1)S(1)}, pred[1,8,4,128]{3,1,2,0:T(8,128)(4,1)}, u32[]{:S(2)}) copy-start(pred[1,8,4,128]{3,1,2,0:T(8,128)(4,1)} %copy-done.69) | copy-start | bytes 12292
  813.0 12.0 copy-start.11
  813.0 12.0 copy-start.44
  813.0 12.0 copy-start.71
  827.9 15.7 copy-start.41
  827.9 203.6 %reduce-scatter.13.cloned.1.call-start = ((), (), s32[]{:S(2)}) async-start(), calls=%async_computation.12 | async-start | bytes 1081344 | tf_op jit(solution)/shard_map/reduce_scatter | solution.py:283
  828.0 15.7 copy-start.86
  828.0 32.9 %slice-start.6 = ((s8[8388608]{0:T(1024)(128)(4,1)}), s8[4194304]{0:T(1024)(128)(4,1)S(1)}, s32[]{:S(2)}) async-start(s8[8388608]{0:T(1024)(128)(4,1)} %bitcast.357), calls=%async_computation.26 | async-start | bytes 8388608
  843.7 14.8 copy-start.39
  843.7 17.2 %slice-start.7 = ((s8[8388608]{0:T(1024)(128)(4,1)}), s8[4194304]{0:T(1024)(128)(4,1)S(1)}, s32[]{:S(2)}) async-start(s8[8388608]{0:T(1024)(128)(4,1)} %bitcast.357), calls=%async_computation.27 | async-start | bytes 8388608
  873.0 19.6 %slice-start = ((s8[8388608]{0:T(1024)(128)(4,1)}), s8[4194304]{0:T(1024)(128)(4,1)S(1)}, s32[]{:S(2)}) async-start(s8[8388608]{0:T(1024)(128)(4,1)} %bitcast.351), calls=%async_computation.20 | async-start | bytes 8388608
  898.7 277.7 %reduce-scatter.19.cloned.1.call-start = ((), (), s32[]{:S(2)}) async-start(), calls=%async_computation.15 | async-start | bytes 147456 | tf_op jit(solution)/shard_map/reduce_scatter | solution.py:289
  902.1 309.5 %reduce-scatter.15.cloned.1.call-start = ((), (), s32[]{:S(2)}) async-start(), calls=%async_computation.13 | async-start | bytes 442368 | tf_op jit(solution)/shard_map/reduce_scatter | solution.py:287
  908.3 337.0 %reduce-scatter.17.cloned.1.call-start = ((), (), s32[]{:S(2)}) async-start(), calls=%async_computation.14 | async-start | bytes 589824 | tf_op jit(solution)/shard_map/reduce_scatter | solution.py:288
  914.2 117.4 %copy-start.65 = (f32[2,2,32,128]{3,2,1,0:T(8,128)S(1)}, f32[2,2,32,128]{3,2,1,0:T(8,128)}, u32[]{:S(2)}) copy-start(f32[2,2,32,128]{3,2,1,0:T(8,128)} %param.46) | copy-start | bytes 196612
  914.2 118.8 %copy-start.68 = (f32[2,32,128]{2,1,0:T(8,128)S(1)}, f32[2,32,128]{2,1,0:T(8,128)}, u32[]{:S(2)}) copy-start(f32[2,32,128]{2,1,0:T(8,128)} %param.40) | copy-start | bytes 98308
  914.2 375.2 %reduce-scatter.21.cloned.1.call-start = ((), (), s32[]{:S(2)}) async-start(), calls=%async_computation.16 | async-start | bytes 589824 | tf_op jit(solution)/shard_map/reduce_scatter | solution.py:290
  920.0 436.3 %all-gather.11.cloned.1.call-start = ((), (), s32[]{:S(2)}) async-start(), calls=%async_computation.19 | async-start | bytes 1310720 | tf_op jit(solution)/shard_map/all_gather | solution.py:309
  954.5 411.3 %all-gather.9.cloned.1.call-start = ((), (), s32[]{:S(2)}) async-start(), calls=%async_computation.18 | async-start | bytes 1081344 | tf_op jit(solution)/shard_map/all_gather | solution.py:301
  1034.4 16.8 %copy-start.31 = (bf16[256,1024]{1,0:T(8,128)(2,1)S(1)}, bf16[256,1024]{1,0:T(8,128)(2,1)}, u32[]{:S(2)}) copy-start(bf16[256,1024]{1,0:T(8,128)(2,1)} %param.34) | copy-start | bytes 1572868
  1034.4 458.1 %reduce-scatter.9.cloned.1.call-start = ((), (), s32[]{:S(2)}) async-start(), calls=%async_computation.9 | async-start | bytes 20971520 | tf_op jit(solution)/shard_map/reduce_scatter | solution.py:233
  1034.4 16.7 %copy-start.9 = (bf16[32,8,4,1024]{3,1,2,0:T(8,128)(2,1)S(1)}, bf16[32,8,4,1024]{3,1,2,0:T(8,128)(2,1)}, u32[]{:S(2)}) copy-start(bf16[32,8,4,1024]{3,1,2,0:T(8,128)(2,1)} %copy-done.8) | copy-start | bytes 6291460
  1065.3 555.7 %reduce-scatter.11.cloned.1.call-start = ((), (), s32[]{:S(2)}) async-start(), calls=%async_computation.11 | async-start | bytes 20971520 | tf_op jit(solution)/shard_map/reduce_scatter | solution.py:280
  1066.3 16.3 slice-start.8
  1111.3 16.4 %copy-start.7 = (f32[4096,128]{1,0:T(8,128)S(1)}, f32[4096,128]{1,0:T(8,128)}, u32[]{:S(2)}) copy-start(f32[4096,128]{1,0:T(8,128)} %copy-done.5) | copy-start | bytes 6291460
  1111.3 16.4 %copy-start.24 = (bf16[2,1024,128]{2,1,0:T(8,128)(2,1)S(1)}, bf16[2,1024,128]{2,1,0:T(8,128)(2,1)}, u32[]{:S(2)}) copy-start(bf16[2,1024,128]{2,1,0:T(8,128)(2,1)} %copy-done.22) | copy-start | bytes 1572868
  1111.3 16.4 %copy-start.48 = (f32[4096]{0:T(1024)S(1)}, f32[4096]{0:T(1024)}, u32[]{:S(2)}) copy-start(f32[4096]{0:T(1024)} %copy-done.47) | copy-start | bytes 49156
  1111.3 16.4 %copy-start.60 = (f32[4096]{0:T(1024)S(1)}, f32[4096]{0:T(1024)}, u32[]{:S(2)}) copy-start(f32[4096]{0:T(1024)} %copy-done.59) | copy-start | bytes 49156
  1111.3 16.4 %copy-start.79 = (f32[1,1024]{1,0:T(1,128)S(1)}, f32[1,1024]{1,0:T(1,128)}, u32[]{:S(2)}) copy-start(f32[1,1024]{1,0:T(1,128)} %copy-done.78) | copy-start | bytes 12292
  1175.7 35.9 %copy-start.61 = (f32[2,16,768]{2,1,0:T(8,128)S(1)}, f32[2,16,768]{2,1,0:T(8,128)}, u32[]{:S(2)}) copy-start(f32[2,16,768]{2,1,0:T(8,128)} %param.47) | copy-start | bytes 294916
  1175.7 36.7 %copy-start.63 = (f32[16,768]{1,0:T(8,128)S(1)}, f32[16,768]{1,0:T(8,128)}, u32[]{:S(2)}) copy-start(f32[16,768]{1,0:T(8,128)} %param.41) | copy-start | bytes 147460
  1175.7 69.6 %copy-start.53 = (f32[2,16,1024]{2,1,0:T(8,128)S(1)}, f32[2,16,1024]{2,1,0:T(8,128)}, u32[]{:S(2)}) copy-start(f32[2,16,1024]{2,1,0:T(8,128)} %param.48) | copy-start | bytes 393220
  1175.7 70.4 %copy-start.56 = (f32[16,1024]{1,0:T(8,128)S(1)}, f32[16,1024]{1,0:T(8,128)}, u32[]{:S(2)}) copy-start(f32[16,1024]{1,0:T(8,128)} %param.42) | copy-start | bytes 196612
  1175.7 113.7 %copy-start.54 = (f32[2,1024,16]{1,2,0:T(8,128)S(1)}, f32[2,1024,16]{1,2,0:T(8,128)}, u32[]{:S(2)}) copy-start(f32[2,1024,16]{1,2,0:T(8,128)} %param.50) | copy-start | bytes 393220
  1175.7 114.5 %copy-start.58 = (f32[1024,16]{0,1:T(8,128)S(1)}, f32[1024,16]{0,1:T(8,128)}, u32[]{:S(2)}) copy-start(f32[1024,16]{0,1:T(8,128)} %param.44) | copy-start | bytes 196612
  1175.7 183.9 %copy-start.27 = (bf16[1024,1024]{1,0:T(8,128)(2,1)S(1)}, bf16[1024,1024]{1,0:T(8,128)(2,1)}, u32[]{:S(2)}) copy-start(bf16[1024,1024]{1,0:T(8,128)(2,1)} %param.36) | copy-start | bytes 6291460
  1365.8 126.7 %copy-start.37 = (bf16[2,128,256]{2,1,0:T(8,128)(2,1)S(1)}, bf16[2,128,256]{2,1,0:T(8,128)(2,1)}, u32[]{:S(2)}) copy-start(bf16[2,128,256]{2,1,0:T(8,128)(2,1)} %copy-done.36) | copy-start | bytes 393220
  1371.7 124.6 %copy-start.43 = (bf16[4096,128]{1,0:T(8,128)(2,1)S(1)}, bf16[4096,128]{1,0:T(8,128)(2,1)}, u32[]{:S(2)}) copy-start(bf16[4096,128]{1,0:T(8,128)(2,1)} %get-tuple-element.181) | copy-start | bytes 3145732
  1371.7 124.6 %copy-start.72 = (pred[1,8,4,128]{3,1,2,0:T(8,128)(4,1)S(1)}, pred[1,8,4,128]{3,1,2,0:T(8,128)(4,1)}, u32[]{:S(2)}) copy-start(pred[1,8,4,128]{3,1,2,0:T(8,128)(4,1)} %copy-done.69) | copy-start | bytes 12292
  1378.2 242.8 %copy-start.12 = (bf16[4096,256]{1,0:T(8,128)(2,1)S(1)}, bf16[4096,256]{1,0:T(8,128)(2,1)}, u32[]{:S(2)}) copy-start(bf16[4096,256]{1,0:T(8,128)(2,1)} %param.29) | copy-start | bytes 6291460
  (55 other events, 327.2 us)
Sparse Core Ops, SparseCore 0:
  9.7 62.0 all-gather.4
  73.4 59.3 all-gather.6
  828.1 59.0 reduce-scatter.22
  898.8 132.6 reduce-scatter.12
  1036.2 56.8 reduce-scatter.18
  1097.1 60.3 reduce-scatter.14
  1162.4 61.2 reduce-scatter.16
  1228.2 61.1 reduce-scatter.20
  1291.0 15.7 all-gather.10
  1310.0 54.1 all-gather.8
  1367.0 125.3 reduce-scatter.8
  1494.9 126.0 reduce-scatter.10
where the time goes:
time: 1640 us; the launch traced here: 1630 us
  blocking collectives  509 us (31%)
  matrix products  503 us (31%)
  waiting for transfers between devices  355 us (22%)
  other arithmetic  134 us (8%)
  local copies, waits for them, and re-layouts  113 us (7%)
    psum x1, blocking collectives, per_device(): lax.psum((product(context_flat, out_rows), product(active, down_rows)), '...  146 us
    dot_general x14, matrix products, cols_product(): lax.dot_general(left_side, right_side, (((1,), (1,)), ((), ())), preferre...  137 us
    reduce_scatter x1, waiting for transfers between devices, per_device(): lax.psum_scatter(mlp_part + attn_part, 'mp', scatter_dimension=1, tiled=T...  121 us
    dot_general x12, matrix products, product(): return jnp.dot(left_side, right_side, preferred_element_type=jnp.float32)  117 us
    reduce_scatter x1, waiting for transfers between devices, per_device(): lax.psum_scatter(product(context_flat, out_weight) + product(active, down...  114 us
    reduce_scatter x1, waiting for transfers between devices, per_device(): lax.psum_scatter(jnp.stack([grad_in_qkv, grad_in_up]), ('dp', 'mp'), scat...  77 us
    dot_general x8, matrix products, masked_scores(): jnp.einsum('qhd,khd->hqk', queries, key_side, preferred_element_type=jnp....  66.9 us
    all_gather x1, blocking collectives, per_device(): lax.all_gather(in_factor.astype(jnp.bfloat16), ('dp', 'mp'), axis=1, tile...  42.9 us
  transfers between devices with their start and end apart: 12, of which 4 were waited for; matrix products, arithmetic and copies ran while one was open for 31% of the time, Pallas kernels for 0%

commit v1 on v0

v1 whole, which is shorter than its diff:
```python
import functools
import math

import jax
import jax.numpy as jnp
from jax import lax
from jax.experimental import pallas as pl
from jax.experimental.pallas import tpu as pltpu
from jax.sharding import PartitionSpec as P

HEAD = 64
ROT = 16
BF = jnp.bfloat16
F32 = jnp.float32

first_fix = 1.0 - math.exp(100.0 * math.log(0.9))
second_fix = 1.0 - math.exp(100.0 * math.log(0.999))


def mm(a, b):
    return lax.dot_general(a, b, (((1,), (0,)), ((), ())), preferred_element_type=F32)


def mm_t(a, b):
    return lax.dot_general(a, b, (((1,), (1,)), ((), ())), preferred_element_type=F32)


def rows_mm(a, b):
    return lax.dot_general(a, b, (((0,), (0,)), ((), ())), preferred_element_type=F32)


def layer_norm(x):
    centred = x - jnp.mean(x, -1, keepdims=True)
    scale = lax.rsqrt(jnp.mean(centred * centred, -1, keepdims=True) + 1e-05)
    return centred * scale, scale


def layer_norm_back(grad_unit, unit_rows, scale):
    return scale * (
        grad_unit
        - jnp.mean(grad_unit, -1, keepdims=True)
        - unit_rows * jnp.mean(grad_unit * unit_rows, -1, keepdims=True)
    )


def rotate(values, cos, sin_a, sin_b, sign):
    width = values.shape[-1]
    turned = pltpu.roll(values, width - ROT // 2, 1) * sin_a + pltpu.roll(values, ROT // 2, 1) * sin_b
    return values * cos + turned if sign > 0 else values * cos - turned


def input_pairs(sizes, core, sources, fin_v, res_places):
    high, folds, ranks, rank, own_cols, direct = sizes
    if not direct:
        f_in, f_res = sources
        return [(f_in, fin_v), (f_res.at[0], res_places[0]), (f_res.at[1], res_places[1])]
    width = 2 * folds * rank + 2 * own_cols
    found = []
    for c in range(2):
        deep, wide2 = sources[c], sources[2 + c]
        which = core if c == 0 else 1 - core
        for y in range(high):
            for n in range(2):
                for j in range(folds):
                    at = y * width + (n * folds + j) * rank
                    rows = pl.ds(pl.multiple_of(((y * 2 + which) * folds + j) * ranks, ranks), ranks)
                    found.append((deep.at[:, :, at : at + rank], fin_v.at[n, :, rows, :]))
                at = y * width + 2 * folds * rank + n * own_cols
                place = pl.ds(pl.multiple_of((y * 2 + which) * own_cols, own_cols), own_cols)
                found.append((wide2.at[:, at : at + own_cols], res_places[n].at[:, place]))
    return found


def block_kernel(cfg, scal, *refs):
    chunk, seqs, first, last, length, tile, parts, cols, dim, wide, units, rank, sizes, n_src = cfg
    whole_rows, refs = refs[:4], refs[4:]
    received, refs = refs[: 2 * parts - 4], refs[2 * parts - 4 :]
    (gain, shift, b_qkv, b_up, rope, w_qkv, w_up, w_down, w_out, f_split), refs = refs[:10], refs[10:]
    sources, refs = refs[:n_src], refs[n_src:]
    (acc_in, res_in, keep, send), refs = refs[:4], refs[4:]
    sums, refs = refs[: len(refs) - 31], refs[len(refs) - 31 :]
    (
        fin_v, gin_b, gres_b, gsplit_b, x_v, c_v, wq_v, wu_v, wd_v, ft_v, rope_v, acc_v, res_v,
        q_s, k_s, v_s, g_s, qt_s, gt_s, gq_s, gkt_s, gvt_s, ac_s, p_s, qr_s, gor_s, out_v,
        row_sems, w_sems, out_sems, acc_sems,
    ) = refs
    me = scal[seqs]
    core = lax.rem(me, 2)
    steps = length // tile
    mixed_cols = 3 * wide
    joint = units + wide

    def tiles_of(s):
        return (scal[s] + tile - 1) // tile

    def row_slice(t, size=tile):
        return pl.ds(pl.multiple_of(t * tile, tile), size)


    def row_copies(s, t):
        found = []
        slot = lax.rem(s, 2)
        for which, dest in enumerate((x_v, c_v)):
            for k in range(parts):
                at = pl.ds(pl.multiple_of(s * length + t * tile, tile), tile)
                if k < 2:
                    src = whole_rows[2 * k + which].at[
                        pl.ds(pl.multiple_of((chunk * seqs + s) * length + t * tile, tile), tile), :
                    ]
                else:
                    src = received[2 * (k - 2) + which].at[at, :]
                place = pl.ds(pl.multiple_of(jnp.bitwise_xor(me, k) * cols, cols), cols)
                found.append(
                    pltpu.make_async_copy(
                        src, dest.at[slot, row_slice(t), place], row_sems.at[slot, t, which * parts + k]
                    )
                )
        return found

    def start_rows(s):
        def one(t, carry):
            for copy in row_copies(s, t):
                copy.start()
            return carry

        lax.fori_loop(0, tiles_of(s), one, 0)

    def out_copies(s, t):
        found = []
        for which in range(2):
            for k in range(parts):
                place = pl.ds(pl.multiple_of(jnp.bitwise_xor(me, k) * cols, cols), cols)
                target = keep if k % 2 == 0 else send
                at = (k // 2) * cols
                rows = pl.ds(pl.multiple_of(s * length + t * tile, tile), tile)
                found.append(
                    pltpu.make_async_copy(
                        out_v.at[which, row_slice(t), place],
                        target.at[which, rows, at : at + cols],
                        out_sems.at[t, which * parts + k],
                    )
                )
        return found

    def drain(s):
        def one(t, carry):
            for copy in out_copies(s, t):
                copy.wait()
            return carry

        lax.fori_loop(0, tiles_of(s), one, 0)

    res_places = (wd_v.at[joint + rank :, :dim], wd_v.at[joint : joint + rank, :dim])
    pairs = [
        (w_qkv, wq_v.at[:dim, :mixed_cols]),
        (f_split.at[:, :mixed_cols], wq_v.at[dim:, :mixed_cols]),
        (rope, rope_v),
        (w_up, wu_v.at[:dim, :units]),
        (f_split.at[:, mixed_cols : mixed_cols + units], wu_v.at[dim:, :units]),
        (w_down, wd_v.at[:units, :dim]),
        (w_out, wd_v.at[units:joint, :dim]),
        (f_split.at[:, mixed_cols + units :], ft_v),
    ] + input_pairs(sizes, core, sources, fin_v, res_places)
    loads = [pltpu.make_async_copy(a, b, w_sems.at[i]) for i, (a, b) in enumerate(pairs)]
    start_rows(0)
    for load in loads:
        load.start()
    back_in = []
    if first:
        acc_v[...] = jnp.zeros_like(acc_v)
        res_v[...] = jnp.zeros_like(res_v)
    else:
        back_in = [
            pltpu.make_async_copy(acc_in, acc_v, acc_sems.at[0]),
            pltpu.make_async_copy(res_in, res_v, acc_sems.at[1]),
        ]
        for copy in back_in:
            copy.start()
    wd_v[:units, dim + rank :] = jnp.zeros((units, rank), BF)
    wd_v[units:joint, dim : dim + rank] = jnp.zeros((wide, rank), BF)
    for load in loads:
        load.wait()
    for copy in back_in:
        copy.wait()
    wd_v[:units, dim : dim + rank] = ft_v[:, :units].astype(F32).T.astype(BF)
    wd_v[units:joint, dim + rank :] = ft_v[:, units:].astype(F32).T.astype(BF)
    wq_v[:dim, mixed_cols:] = fin_v[0].reshape(dim, rank)
    wu_v[:dim, units:] = fin_v[1].reshape(dim, rank)

    def whole(ref, top, depth, width, cut, other, at):
        def one(i, carry):
            rows = pl.ds(pl.multiple_of(top + i * cut, cut), cut)
            low_rank = mm(ref[rows, at : at + rank], other())
            ref[rows, :width] = (ref[rows, :width].astype(F32) + low_rank).astype(BF)
            return carry

        lax.fori_loop(0, depth // cut, one, 0)

    cut = min(256, units, wide)
    whole(wu_v, 0, dim, units, cut, lambda: wu_v[dim:, :units], units)
    whole(wd_v, 0, units, dim, cut, lambda: wd_v[joint : joint + rank, :dim], dim)
    whole(wd_v, units, wide, dim, cut, lambda: wd_v[joint + rank :, :dim], dim + rank)

    c_in0, c_in1, c_qkv, c_up, c_down, c_out = (
        slice(0, dim),
        slice(dim, 2 * dim),
        slice(2 * dim, 2 * dim + mixed_cols),
        slice(2 * dim + mixed_cols, 2 * dim + mixed_cols + units),
        slice(2 * dim + mixed_cols + units, 2 * dim + mixed_cols + 2 * units),
        slice(2 * dim + mixed_cols + 2 * units, 2 * dim + mixed_cols + 2 * units + wide),
    )
    lane = lax.broadcasted_iota(jnp.int32, (1, 128), 1)
    left = lane < HEAD

    def one_sequence(s, carry):
        seq_len = scal[s]
        count = tiles_of(s)
        slot = lax.rem(s, 2)

        @pl.when(s + 1 < seqs)
        def _():
            start_rows(s + 1)

        gkt_s[...] = jnp.zeros_like(gkt_s)
        gvt_s[...] = jnp.zeros_like(gvt_s)

        def upstream(t, size):
            position = t * tile + lax.broadcasted_iota(jnp.int32, (size, 1), 0)
            return jnp.where(position < seq_len, c_v[slot, row_slice(t, size), :].astype(F32), 0.0).astype(BF)

        def tables(t, size):
            rows = row_slice(t, size)
            return [jnp.concatenate([rope_v[i, rows, :]] * (wide // 128), 1) for i in range(3)]

        def forward(t, size):
            rows = row_slice(t, size)
            for j in range(size // tile):
                for copy in row_copies(s, t + j):
                    copy.wait()
            unit, _ = layer_norm(x_v[slot, rows, :].astype(F32))
            low_one = (unit * gain[0:1, :] + shift[0:1, :]).astype(BF)
            low_two = (unit * gain[1:2, :] + shift[1:2, :]).astype(BF)
            ups = upstream(t, size)
            hidden = mm(low_two, wu_v[:dim, :])
            back = mm_t(ups, wd_v[:, :dim])
            mixed = mm(low_one, wq_v[:dim, :])
            code_up = hidden[:, units:]
            hidden = hidden[:, :units] + b_up[...]
            code_qkv = mixed[:, mixed_cols:]
            mixed = mixed[:, :mixed_cols] + mm(code_qkv.astype(BF), wq_v[dim:, :mixed_cols]) + b_qkv[...]
            blocks = [mixed[:, i * 128 : (i + 1) * 128] for i in range(mixed_cols // 128)]
            cat = lambda found: jnp.concatenate(found, 1) if len(found) > 1 else found[0]
            q_mixed = cat([jnp.where(left, blocks[3 * p], blocks[3 * p + 1]) for p in range(wide // 128)])
            k_mixed = cat(
                [pltpu.roll(jnp.where(left, blocks[3 * p + 2], blocks[3 * p]), HEAD, 1) for p in range(wide // 128)]
            )
            v_mixed = cat([jnp.where(left, blocks[3 * p + 1], blocks[3 * p + 2]) for p in range(wide // 128)])
            cdf = 0.5 * (1.0 + lax.erf(hidden * (1.0 / math.sqrt(2.0))))
            active = (hidden * cdf).astype(BF)
            slope = cdf + hidden * (jnp.exp(-0.5 * hidden * hidden) * (1.0 / math.sqrt(2.0 * math.pi)))
            grad_hidden = (back[:, :units] * slope).astype(BF)
            ac_s[rows, :units] = active
            cos, sin_a, sin_b = tables(t, size)
            query = rotate(q_mixed, cos, sin_a, sin_b, 1).astype(BF).astype(F32) * HEAD**-0.5
            q_s[rows, :] = query.astype(BF)
            qt_s[:, rows] = query.T.astype(BF)
            k_s[rows, :] = rotate(k_mixed, cos, sin_a, sin_b, 1).astype(BF)
            v_s[rows, :] = v_mixed.astype(BF)
            qr_s[:, rows] = code_qkv.T.astype(BF)
            grad_context = back[:, units:joint]
            g_s[rows, :] = grad_context.astype(BF)
            gt_s[:, rows] = grad_context.T.astype(BF)
            gor_s[:, rows] = back[:, joint + rank :].T.astype(BF)
            below = mm_t(grad_hidden, wu_v[:, :units])
            p_s[rows, :] = below[:, :dim] * gain[1:2, :]
            acc_v[:, c_up] += mm(code_up.T.astype(BF), grad_hidden)
            acc_v[:, c_down] += mm(back[:, joint : joint + rank].T.astype(BF), active)
            acc_v[:, c_in1] += mm(below[:, dim:].T.astype(BF), low_two)

        def finish(t, size):
            rows = row_slice(t, size)
            cos, sin_a, sin_b = tables(t, size)
            grad_q = rotate(gq_s[rows, :], cos, sin_a, sin_b, -1)
            grad_k = rotate(gkt_s[:, rows].T, cos, sin_a, sin_b, -1)
            grad_v = gvt_s[:, rows].T
            blocks = []
            for p in range(wide // 128):
                pair = slice(p * 128, (p + 1) * 128)
                one_q, one_k, one_v = grad_q[:, pair], pltpu.roll(grad_k[:, pair], HEAD, 1), grad_v[:, pair]
                blocks += [jnp.where(left, one_q, one_k), jnp.where(left, one_v, one_q), jnp.where(left, one_k, one_v)]
            grad_mixed = jnp.concatenate(blocks, 1).astype(BF)
            below = mm_t(grad_mixed, wq_v[:, :mixed_cols])
            both = ac_s[rows, :]
            ahead = mm(both, wd_v[:joint, :])
            unit, scale = layer_norm(x_v[slot, rows, :].astype(F32))
            low_one = (unit * gain[0:1, :] + shift[0:1, :]).astype(BF)
            out_v[0, rows, :] = ahead[:, :dim].astype(BF)
            grad_code = below[:, dim:]
            grad_norm = below[:, :dim] + mm_t(grad_code.astype(BF), wq_v[:dim, mixed_cols:])
            grad_unit = grad_norm * gain[0:1, :] + p_s[rows, :]
            out_v[1, rows, :] = layer_norm_back(grad_unit, unit, scale).astype(BF)
            for j in range(size // tile):
                for copy in out_copies(s, t + j):
                    copy.start()
            acc_v[:, c_in0] += mm(grad_code.T.astype(BF), low_one)
            acc_v[:, c_qkv] += mm(qr_s[:, rows], grad_mixed)
            acc_v[:, c_out] += mm(gor_s[:, rows], both[:, units:])
            res_v[...] += mm(ahead[:, dim:].T.astype(BF), upstream(t, size))

        def over_rows(work):
            def single(j, carry):
                work(j, tile)
                return carry

            lax.fori_loop(0, count, single, 0)

        over_rows(forward)

        for i in range(steps):
            @pl.when(i < count)
            def _(i=i):
                qrows = pl.ds(i * tile, tile)
                before, extent = i * tile, (i + 1) * tile
                qpos = before + lax.broadcasted_iota(jnp.int32, (tile, tile), 0)
                kpos = before + lax.broadcasted_iota(jnp.int32, (tile, tile), 1)
                allowed = (kpos <= qpos) & (kpos < seq_len)
                allowed = jnp.concatenate([allowed, allowed], 0)
                def one_pair(p, carry):
                    pair = pl.ds(pl.multiple_of(p * 128, 128), 128)
                    q_all, g_all = q_s[qrows, pair], g_s[qrows, pair]
                    zero = jnp.zeros_like(q_all)
                    q_two = jnp.concatenate([jnp.where(left, q_all, zero), jnp.where(left, zero, q_all)], 0)
                    g_two = jnp.concatenate([jnp.where(left, g_all, zero), jnp.where(left, zero, g_all)], 0)
                    keys, vals = k_s[:extent, pair], v_s[:extent, pair]
                    scores = mm_t(q_two, keys)
                    grad_probs = mm_t(g_two, vals)
                    last = jnp.where(allowed, scores[:, before:], -1e30)
                    scores = jnp.concatenate([scores[:, :before], last], 1) if i else last
                    weights = jnp.exp(scores - jnp.max(scores, -1, keepdims=True))
                    probs = weights * (1.0 / jnp.sum(weights, -1, keepdims=True))
                    low_probs = probs.astype(BF)
                    context = mm(low_probs, vals)
                    row_term = jnp.sum(probs * grad_probs, -1, keepdims=True)
                    grad_scores = (probs * (grad_probs - row_term)).astype(BF)
                    grad_q = mm(grad_scores, keys)
                    ac_s[qrows, pl.ds(pl.multiple_of(units + p * 128, 128), 128)] = jnp.where(
                        left, context[:tile], context[tile:]
                    ).astype(BF)
                    gq_s[qrows, pair] = jnp.where(left, grad_q[:tile], grad_q[tile:]) * HEAD**-0.5
                    for h in range(2):
                        feats = pl.ds(pl.multiple_of(p * 128 + h * HEAD, HEAD), HEAD)
                        part = slice(h * tile, (h + 1) * tile)
                        gkt_s[feats, :extent] += mm(qt_s[feats, qrows], grad_scores[part])
                        gvt_s[feats, :extent] += mm(gt_s[feats, qrows], low_probs[part])
                    return carry

                lax.fori_loop(0, wide // 128, one_pair, 0)

        @pl.when(s > 0)
        def _():
            drain(s - 1)

        over_rows(finish)
        return carry

    lax.fori_loop(0, seqs, one_sequence, 0)
    if not last:
        targets = [(acc_v, sums[0]), (res_v, sums[1])]
    else:
        high, folds, ranks, _, own_cols, direct = sizes
        gsplit_b[...] = acc_v[:, 2 * dim :].astype(BF)
        gres_b[:rank, :] = res_v[rank:, :].astype(BF)
        gres_b[rank:, :] = res_v[:rank, :].astype(BF)
        for n, place in enumerate((c_in0, c_in1)):
            gin_b[n] = acc_v[:, place].T.astype(BF).reshape(gin_b.shape[1:])
        targets = [(gsplit_b, sums[0])]
        if not direct:
            targets += [(gin_b, sums[1]), (gres_b, sums[2])]
        else:
            for c in range(2):
                which = core if c == 0 else 1 - core
                for y in range(high):
                    for n in range(2):
                        for j in range(folds):
                            at = (n * folds + j) * rank
                            rows = pl.ds(pl.multiple_of(((y * 2 + which) * folds + j) * ranks, ranks), ranks)
                            targets.append((gin_b.at[n, :, rows, :], sums[1 + c].at[y, :, :, at : at + rank]))
                        place = pl.ds(pl.multiple_of((y * 2 + which) * own_cols, own_cols), own_cols)
                        targets.append(
                            (gres_b.at[n * rank : (n + 1) * rank, place],
                             sums[3 + c].at[y, :, n * own_cols : (n + 1) * own_cols])
                        )
    back_out = [pltpu.make_async_copy(a, b, acc_sems.at[2 + i]) for i, (a, b) in enumerate(targets)]
    for copy in back_out:
        copy.start()
    drain(seqs - 1)
    for copy in back_out:
        copy.wait()


def block_call(chunk, seqs, last, sizes, acc, scal, whole_rows, received, small, weights, factors, length, parts):
    gain, shift, b_qkv, b_up, rope = small
    w_qkv, w_up, w_down, w_out = weights
    f_split, sources = factors
    dim, units, wide, rank = w_up.shape[0], w_up.shape[1], w_out.shape[0], f_split.shape[0]
    high, folds, ranks, _, own_cols, direct = sizes
    dp = rank // ranks
    cols = dim // parts
    tile = 256 if length % 256 == 0 else 128
    steps = length // tile
    first = acc is None
    acc_shape = jax.ShapeDtypeStruct((rank, 2 * dim + 4 * wide + 2 * units), F32)
    res_shape = jax.ShapeDtypeStruct((2 * rank, dim), F32)
    if first:
        acc = (jnp.zeros((8, 128), F32), jnp.zeros((8, 128), F32))
    cfg = (chunk, seqs, first, last, length, tile, parts, cols, dim, wide, units, rank, sizes, len(sources))
    ANY = pl.BlockSpec(memory_space=pl.ANY)
    VM = pl.BlockSpec(memory_space=pltpu.VMEM)
    operands = [scal, *whole_rows, *received, gain, shift, b_qkv, b_up, rope, *weights, f_split, *sources, *acc]
    specs = [pl.BlockSpec(memory_space=pltpu.SMEM)] + [ANY] * (2 * parts) + [VM] * 4 + [ANY] * (8 + len(sources))
    flops = 2 * seqs * length * (dim * (units * 4 + wide * 8 + rank * 12) + units * rank * 6 + length * wide * 12)
    out = jax.ShapeDtypeStruct((2, seqs * length, dim // 2), BF)
    if not last:
        sums = [acc_shape, res_shape]
    else:
        sums = [jax.ShapeDtypeStruct((rank, 4 * wide + 2 * units), BF)]
        if direct:
            sums += [jax.ShapeDtypeStruct((high, dp, ranks, 2 * folds * rank), BF)] * 2
            sums += [jax.ShapeDtypeStruct((high, rank, 2 * own_cols), BF)] * 2
        else:
            sums += [jax.ShapeDtypeStruct((2, dp, dim // dp, rank), BF), jax.ShapeDtypeStruct((2 * rank, dim), BF)]
    in_shape = (2, dp, dim // dp, rank)
    tall = lambda n, dtype: pltpu.VMEM((length, n), dtype)
    flat = lambda n, dtype: pltpu.VMEM((n, length), dtype)
    return pl.pallas_call(
        functools.partial(block_kernel, cfg),
        out_shape=[out, out, *sums],
        in_specs=specs,
        out_specs=[ANY] * (2 + len(sums)),
        scratch_shapes=[
            pltpu.VMEM(in_shape, BF),
            pltpu.VMEM(in_shape if last else (2, 1, 16, rank), BF),
            pltpu.VMEM((2 * rank, dim) if last else (16, 128), BF),
            pltpu.VMEM((rank, 4 * wide + 2 * units) if last else (16, 128), BF),
            pltpu.VMEM((2, length, dim), BF),
            pltpu.VMEM((2, length, dim), BF),
            pltpu.VMEM((dim + rank, 3 * wide + rank), BF),
            pltpu.VMEM((dim + rank, units + rank), BF),
            pltpu.VMEM((units + wide + 2 * rank, dim + 2 * rank), BF),
            pltpu.VMEM((rank, units + wide), BF),
            pltpu.VMEM(rope.shape, F32),
            pltpu.VMEM(acc_shape.shape, F32),
            pltpu.VMEM(res_shape.shape, F32),
            tall(wide, BF), tall(wide, BF), tall(wide, BF), tall(wide, BF),
            flat(wide, BF), flat(wide, BF),
            tall(wide, F32), flat(wide, F32), flat(wide, F32),
            tall(units + wide, BF), tall(dim, F32),
            flat(rank, BF), flat(rank, BF),
            pltpu.VMEM((2, length, dim), BF),
            pltpu.SemaphoreType.DMA((2, steps, 2 * parts)),
            pltpu.SemaphoreType.DMA((8 + (4 * high * (folds + 1) if direct else 3),)),
            pltpu.SemaphoreType.DMA((steps, 2 * parts)),
            pltpu.SemaphoreType.DMA((5 + 4 * high * (folds + 1),)),
        ],
        input_output_aliases={} if first or last else {len(operands) - 2: 2, len(operands) - 1: 3},
        compiler_params=pltpu.CompilerParams(vmem_limit_bytes=60 * 1024 * 1024),
        cost_estimate=pl.CostEstimate(
            flops=2 * flops, bytes_accessed=32 * 1024 * 1024, transcendentals=2 * seqs * length * units
        ),
        name="block",
    )(*operands)


def finish_kernel(cfg, lens, *refs):
    terms, block, length, aliased = cfg
    parts, refs = refs[:terms], refs[terms:]
    tokens, cotangent, bias = refs[:3]
    result, grad = refs[-2:]
    at = pl.program_id(0) * block
    seq_len = lens[at // length]
    position = at % length + lax.broadcasted_iota(jnp.int32, (block, 1), 0)
    valid = position < seq_len
    total = sum(part[...].astype(F32) for part in parts)
    result[...] = jnp.where(valid, tokens[...].astype(F32) + total[0] + bias[0:1, :] + bias[1:2, :], 0.0)
    grad[...] = jnp.where(valid, cotangent[...].astype(F32) + total[1], 0.0)


def finish_call(chunk, lens, parts, tokens, cotangent, bias, length, earlier):
    rows, cols = tokens.shape
    span = parts[0].shape[1]
    block = min(512, length)
    base = chunk * span // block
    part_spec = pl.BlockSpec((2, block, cols), lambda i: (0, i, 0))
    row_spec = pl.BlockSpec((block, cols), lambda i: (base + i, 0))
    specs = [pl.BlockSpec(memory_space=pltpu.SMEM)] + [part_spec] * len(parts) + [row_spec] * 2
    specs += [pl.BlockSpec(bias.shape, lambda i: (0, 0))] + [pl.BlockSpec(memory_space=pl.ANY)] * len(earlier)
    operands = [lens, *parts, tokens, cotangent, bias, *earlier]
    return pl.pallas_call(
        functools.partial(finish_kernel, (len(parts), block, length, bool(earlier))),
        grid=(span // block,),
        out_shape=[jax.ShapeDtypeStruct((rows, cols), F32)] * 2,
        in_specs=specs,
        out_specs=[row_spec] * 2,
        input_output_aliases={len(operands) - 2: 0, len(operands) - 1: 1} if earlier else {},
        cost_estimate=pl.CostEstimate(flops=8 * span * cols, bytes_accessed=20 * span * cols, transcendentals=0),
        name="finish",
    )(*operands)


def merge_kernel(cfg, scal, *refs):
    sizes, dim, wide, units, rank, n_src, cut = cfg
    (w_qkv, w_up, w_down, w_out, f_split), refs = refs[:5], refs[5:]
    sources, refs = refs[:n_src], refs[n_src:]
    outs, refs = refs[:4], refs[4:]
    weights_v, outs_v, (fin_v, res0_v, res1_v, split_v, t_v, in_sems, out_sems) = refs[:4], refs[4:8], refs[8:]
    core = lax.rem(scal[0], 2)
    pairs = input_pairs(sizes, core, sources, fin_v, (res0_v, res1_v)) + [(f_split, split_v)]
    pairs += list(zip((w_qkv, w_up, w_down, w_out), weights_v))
    loads = [pltpu.make_async_copy(a, b, in_sems.at[i]) for i, (a, b) in enumerate(pairs)]
    for load in loads:
        load.start()
    for load in loads:
        load.wait()
    mixed = 3 * wide
    t_v[...] = split_v[:, mixed + units :].astype(F32).T.astype(BF)
    plans = [
        (0, dim, lambda rows: fin_v[0].reshape(dim, rank)[rows], lambda: split_v[:, :mixed]),
        (1, dim, lambda rows: fin_v[1].reshape(dim, rank)[rows], lambda: split_v[:, mixed : mixed + units]),
        (2, units, lambda rows: t_v[rows, :], lambda: res1_v[...]),
        (3, wide, lambda rows: t_v[units + rows.start : units + rows.stop, :], lambda: res0_v[...]),
    ]
    stores = []
    for which, depth, left, right in plans:
        for at in range(0, depth, cut):
            rows = slice(at, at + cut)
            outs_v[which][rows, :] = weights_v[which][rows, :].astype(F32) + mm(left(rows), right())
            copy = pltpu.make_async_copy(outs_v[which].at[rows, :], outs[which].at[rows, :], out_sems.at[len(stores)])
            copy.start()
            stores.append(copy)
    for copy in stores:
        copy.wait()


def merge_call(scal, weights, f_split, sources, sizes, dp):
    w_qkv, w_up, w_down, w_out = weights
    dim, units, wide, rank = w_up.shape[0], w_up.shape[1], w_out.shape[0], f_split.shape[0]
    high, folds, ranks, _, own_cols, direct = sizes
    cut = min(256, wide)
    ANY = pl.BlockSpec(memory_space=pl.ANY)
    chunks = (2 * dim + units + wide) // cut
    return pl.pallas_call(
        functools.partial(merge_kernel, (sizes, dim, wide, units, rank, len(sources), cut)),
        out_shape=[jax.ShapeDtypeStruct(w.shape, F32) for w in weights],
        in_specs=[pl.BlockSpec(memory_space=pltpu.SMEM)] + [ANY] * (5 + len(sources)),
        out_specs=[ANY] * 4,
        scratch_shapes=[pltpu.VMEM(w.shape, BF) for w in weights]
        + [pltpu.VMEM(w.shape, F32) for w in weights]
        + [
            pltpu.VMEM((2, dp, dim // dp, rank), BF),
            pltpu.VMEM((rank, dim), BF),
            pltpu.VMEM((rank, dim), BF),
            pltpu.VMEM(f_split.shape, BF),
            pltpu.VMEM((units + wide, rank), BF),
            pltpu.SemaphoreType.DMA((5 + (4 * high * (folds + 1) if direct else 3),)),
            pltpu.SemaphoreType.DMA((chunks,)),
        ],
        compiler_params=pltpu.CompilerParams(vmem_limit_bytes=40 * 1024 * 1024),
        cost_estimate=pl.CostEstimate(
            flops=2 * rank * (dim * (3 * wide + 2 * units + wide)), bytes_accessed=20 * 1024 * 1024, transcendentals=0
        ),
        name="merge",
    )(scal, *weights, f_split, *sources)


def bits_of(size):
    return [1 << b for b in range(size.bit_length() - 1)]


def swap(x, axis, size, bit):
    return lax.ppermute(x, axis, [(i, i ^ bit) for i in range(size)])


def bit_value(axis, bit):
    return (lax.axis_index(axis) // bit) % 2


def halve(x, axis, size, bit):
    mine = bit_value(axis, bit)
    keep = lax.dynamic_index_in_dim(x, mine, 0, keepdims=False).astype(F32)
    give = lax.dynamic_index_in_dim(x, 1 - mine, 0, keepdims=False).astype(BF)
    return keep + swap(give, axis, size, bit).astype(F32)


def after(x, *earlier):
    return lax.optimization_barrier((x, earlier))[0]


def in_order(x, other, axis, bit):
    upper = bit_value(axis, bit) == 1
    return jnp.where(upper, other, x), jnp.where(upper, x, other)


def spread_inputs(low_in, low_res, mp, wait=()):
    own_rows, rank = low_in.shape[1:]
    own_ranks = low_res.shape[1]
    both = jnp.concatenate(
        [low_in[n, j * own_ranks : (j + 1) * own_ranks] for n in range(2) for j in range(own_rows // own_ranks)]
        + [low_res[0], low_res[1]],
        1,
    )
    if wait:
        both = after(both, *wait)
    for bit in bits_of(mp)[1:]:
        both = jnp.concatenate(in_order(both, swap(both, "mp", mp, bit), "mp", bit), 1)
    return both


def gather_rows(x, dp):
    found = lax.all_to_all(jnp.broadcast_to(x[None], (dp,) + x.shape), "dp", 0, 0, tiled=True)
    return found.reshape(dp * x.shape[0], x.shape[1])


def gather_inputs(both, sizes, dim, dp, mp):
    high, folds, ranks, rank, own_cols, direct = sizes
    found = gather_rows(both, dp)
    other = swap(found, "mp", mp, 1)
    if direct:
        deep = lambda x: x.reshape(dp, ranks, x.shape[1])
        return [deep(found), deep(other), found, other]
    cores = jnp.stack(in_order(found, other, "mp", 1)).reshape(2, dp, ranks, high, both.shape[1] // high)
    in_part = cores[..., : 2 * folds * rank].reshape(2, dp, ranks, high, 2, folds, rank)
    res_part = cores[..., 2 * folds * rank :].reshape(2, dp, ranks, high, 2, own_cols)
    whole_in = in_part.transpose(4, 1, 3, 0, 5, 2, 6).reshape(2, dp, dim // dp, rank)
    return [whole_in, res_part.transpose(4, 1, 2, 3, 0, 5).reshape(2, rank, dim)]


def reduce_inputs(sums, sizes, dim, dp, mp):
    high, folds, ranks, rank, own_cols, direct = sizes
    if direct:
        in_keep, in_send, res_keep, res_send = sums
        in_both = in_keep.astype(F32) + swap(in_send, "mp", mp, 1).astype(F32)
        res_both = res_keep.astype(F32) + swap(res_send, "mp", mp, 1).astype(F32)
        both = jnp.concatenate([in_both.reshape(high, rank, -1), res_both], 2)
    else:
        in_part = sums[0].reshape(2, dp, high, 2, folds, ranks, rank)
        in_part = in_part.transpose(3, 2, 1, 5, 0, 4, 6).reshape(2, high, rank, 2 * folds * rank)
        res_part = sums[1].reshape(2, rank, high, 2, own_cols).transpose(3, 2, 1, 0, 4)
        both = halve(jnp.concatenate([in_part, res_part.reshape(2, high, rank, 2 * own_cols)], 3), "mp", mp, 1)
    both = both.reshape((2,) * len(bits_of(high)) + both.shape[1:])
    for bit in reversed(bits_of(mp)[1:]):
        both = halve(both, "mp", mp, bit)
    return both


def reduce_rows(x, dp):
    return jnp.sum(lax.all_to_all(x.reshape(dp, -1, x.shape[1]), "dp", 0, 0, tiled=True).astype(F32), 0)


def adam_step(factor, moment, gradient):
    first_moment = 0.9 * moment[0] + 0.1 * gradient
    second_moment = 0.999 * moment[1] + 0.001 * gradient * gradient
    updated = factor - 0.01 * (first_moment / first_fix) / (
        jnp.sqrt(second_moment / second_fix) + 1e-08
    )
    keep_mask = (jnp.abs(moment[0]) >= 0.5).astype(F32)
    return (updated, jnp.stack([first_moment * keep_mask, second_moment * keep_mask]))


def rope_tables(length):
    half = ROT // 2
    frequency = 10000.0 ** (-jnp.arange(half, dtype=F32) * 2.0 / ROT)
    angles = jnp.arange(length, dtype=F32)[:, None] * frequency[None, :]
    cos, sin = jnp.cos(angles), jnp.sin(angles)
    ones, zeros = jnp.ones((length, HEAD - ROT), F32), jnp.zeros((length, HEAD - ROT), F32)
    blank = jnp.zeros_like(sin)
    one_head = [
        jnp.concatenate([cos, cos, ones], 1),
        jnp.concatenate([-sin, blank, zeros], 1),
        jnp.concatenate([blank, sin, zeros], 1),
    ]
    return jnp.stack([jnp.concatenate([table, table], 1) for table in one_head])


def per_device(
    dp,
    mp,
    tokens,
    cotangent,
    lengths,
    norm_gain,
    norm_shift,
    qkv_weight,
    out_weight,
    up_weight,
    down_weight,
    qkv_bias,
    up_bias,
    res_bias,
    in_factor,
    qkv_factor,
    up_factor,
    out_factor,
    down_factor,
    res_factor,
    in_moments,
    qkv_moments,
    up_moments,
    out_moments,
    down_moments,
    res_moments,
):
    row_count, cols = tokens.shape
    seq_count = lengths.shape[0]
    length = row_count // seq_count
    wide = out_weight.shape[0]
    dim, units = up_weight.shape
    me = lax.axis_index("mp").astype(jnp.int32)
    mp_bits = bits_of(mp)
    seqs = 2 if seq_count % 2 == 0 else 1
    chunks = seq_count // seqs
    span = seqs * length

    rank = in_factor.shape[2]
    low = lambda f: f.astype(BF)
    both = spread_inputs(low(in_factor), low(res_factor), mp)

    own_ranks, own_cols = res_factor.shape[1:]
    sizes = (mp // 2, in_factor.shape[1] // own_ranks, own_ranks, rank, own_cols, own_ranks % 16 == 0)
    rank_rows = lambda qkv, up, down, out: jnp.concatenate([low(qkv), low(up), low(down).T, low(out).T], 1)
    f_split = gather_rows(rank_rows(qkv_factor, up_factor, down_factor, out_factor), dp)
    sources = gather_inputs(both, sizes, dim, dp, mp)
    whole_rows = (tokens, cotangent, swap(tokens, "mp", mp, 1), swap(cotangent, "mp", mp, 1))

    def far_rows(c, wait):
        held = {0: [tokens[c * span : (c + 1) * span], cotangent[c * span : (c + 1) * span]]}
        for bit in reversed(mp_bits[1:]):
            for k in list(held):
                held[k | bit] = [swap(after(x, *wait), "mp", mp, bit) for x in held[k]]
        return {k: v for k, v in held.items() if k}

    def near_rows(held, wait):
        for k in list(held):
            held[k | 1] = [swap(after(x, *wait) if wait else x, "mp", mp, 1) for x in held[k]]
        return [x for k in sorted(held) for x in held[k]]

    small = (norm_gain, norm_shift, qkv_bias[None], up_bias[None], rope_tables(length))
    marks = [3 * wide, 3 * wide + units, 3 * wide + 2 * units]

    def pieces(packed):
        return jnp.split(packed, marks, 1)

    weights = (qkv_weight, up_weight, down_weight, out_weight)

    def near_sums(keep, send):
        other = swap(send, "mp", mp, 1)
        column = lambda x, j: x[:, :, j * cols : (j + 1) * cols]
        held = {2 * j: [column(keep, j), column(other, j)] for j in range(mp // 2)}
        held[0] = [keep, other]
        return held

    def far_gives(held, bit):
        gone = [k for k in held if k & bit]
        return gone, jnp.concatenate([sum(x.astype(F32) for x in held[k]).astype(BF) for k in gone], 0)

    def far_sums(held, first_give, wait):
        for bit in mp_bits[1:]:
            gone, give = first_give if bit == 2 else far_gives(held, bit)
            moved = swap(after(give, *wait) if wait else give, "mp", mp, bit)
            wait = (moved,)
            for j, k in enumerate(gone):
                held[k ^ bit].append(moved[2 * j : 2 * j + 2])
                del held[k]
        return held[0], wait

    acc = None
    partials, totals = [], []
    far = far_rows(0, (both,))
    for c in range(chunks):
        scal = jnp.concatenate([lengths[c * seqs : (c + 1) * seqs], me[None]])
        wait = () if c == 0 else (partials[-1][0],)
        received = near_rows(far, wait)
        if c + 1 < chunks:
            far = far_rows(c + 1, (received[-1], sources[-1], f_split))
        keep, send, *acc = block_call(
            c, seqs, c == chunks - 1, sizes, acc, scal, whole_rows, received, small, weights,
            (f_split, sources), length, mp,
        )
        partials.append((keep, send))

    split_sum, *input_sums = acc
    grads_both = reduce_inputs(input_sums, sizes, dim, dp, mp)
    wait = (grads_both,)
    for c in range(chunks - 1):
        held = near_sums(*partials[c])
        give = far_gives(held, 2)
        split_sum = after(split_sum, give[1])
        total, wait = far_sums(held, give, wait)
        totals.append(total)
    split_grad = reduce_rows(split_sum, dp)
    own_both = reduce_rows(grads_both.astype(BF), dp)
    own_both, split_grad = after((own_both, split_grad), *wait)
    held = near_sums(*partials[-1])
    last_give = far_gives(held, 2)
    cut = own_both.shape[1] - 2 * own_cols
    in_grad = own_both[:, :cut].reshape(own_ranks, 2, -1, rank).transpose(1, 2, 0, 3).reshape(in_factor.shape)
    res_grad = jnp.stack([own_both[:, cut : cut + own_cols], own_both[:, cut + own_cols :]])
    qkv_owned, up_owned, down_owned, out_owned = pieces(split_grad)
    down_owned, out_owned = down_owned.T, out_owned.T
    new_in, in_pruned = adam_step(in_factor, in_moments, in_grad)
    new_qkv, qkv_pruned = adam_step(qkv_factor, qkv_moments, qkv_owned)
    new_up, up_pruned = adam_step(up_factor, up_moments, up_owned)
    new_out, out_pruned = adam_step(out_factor, out_moments, out_owned)
    new_down, down_pruned = adam_step(down_factor, down_moments, down_owned)
    new_res, res_pruned = adam_step(res_factor, res_moments, res_grad)
    both = spread_inputs(low(new_in), low(new_res), mp)
    total, _ = far_sums(held, last_give, (both,))
    totals.append(total)
    split_whole = gather_rows(rank_rows(new_qkv, new_up, new_down, new_out), dp)
    merged_qkv, merged_up, merged_down, merged_out = merge_call(
        me[None], weights, split_whole, gather_inputs(both, sizes, dim, dp, mp), sizes, dp
    )
    ended = []
    for c in range(chunks):
        ended = finish_call(
            c, lengths[c * seqs : (c + 1) * seqs], totals[c], tokens, cotangent, res_bias, length, ended
        )
    result, grad_tokens = ended
    return (
        result,
        grad_tokens,
        in_grad,
        qkv_owned,
        up_owned,
        out_owned,
        down_owned,
        res_grad,
        merged_qkv,
        merged_out,
        merged_up,
        merged_down,
        in_pruned,
        qkv_pruned,
        up_pruned,
        out_pruned,
        down_pruned,
        res_pruned,
    )


def solution(mesh):
    placed = (
        P("dp", "mp"),
        P("dp", "mp"),
        P("dp"),
        P(),
        P(),
        P(None, "mp"),
        P("mp", None),
        P(None, "mp"),
        P("mp", None),
        P("mp"),
        P("mp"),
        P(None, "mp"),
        P(None, ("dp", "mp"), None),
        P("dp", "mp"),
        P("dp", "mp"),
        P("mp", "dp"),
        P("mp", "dp"),
        P(None, "dp", "mp"),
        P(None, None, ("dp", "mp"), None),
        P(None, "dp", "mp"),
        P(None, "dp", "mp"),
        P(None, "mp", "dp"),
        P(None, "mp", "dp"),
        P(None, None, "dp", "mp"),
    )
    return jax.shard_map(
        functools.partial(per_device, mesh.shape["dp"], mesh.shape["mp"]),
        mesh=mesh,
        in_specs=placed,
        out_specs=(
            P("dp", "mp"),
            P("dp", "mp"),
            P(None, ("dp", "mp"), None),
            P("dp", "mp"),
            P("dp", "mp"),
            P("mp", "dp"),
            P("mp", "dp"),
            P(None, "dp", "mp"),
            P(None, "mp"),
            P("mp", None),
            P(None, "mp"),
            P("mp", None),
            P(None, None, ("dp", "mp"), None),
            P(None, "dp", "mp"),
            P(None, "dp", "mp"),
            P(None, "mp", "dp"),
            P(None, "mp", "dp"),
            P(None, None, "dp", "mp"),
        ),
        check_vma=False,
    )
```

time: 1640 us -> 365 us (0.22)
  blocking collectives: 509 us -> 0 us
  matrix products: 503 us -> 0 us
  waiting for transfers between devices: 355 us -> 95.7 us
  Pallas kernels: 0 us -> 141 us
  other arithmetic: 134 us -> 32.8 us
  local copies, waits for them, and re-layouts: 113 us -> 17.4 us
  starting transfers between devices: 0.49 us -> 70.8 us
    dot_general x68 -> x0, matrix products: 503 us -> none  [the longest x14 137 us: cols_product(): lax.dot_general(left_side, right_side, (((1,), (1,)), ((), ())), preferre...]
    all_gather x11 -> x0, blocking collectives: 363 us -> none  [the longest x1 42.9 us: per_device(): lax.all_gather(in_factor.astype(jnp.bfloat16), ('dp', 'mp'), axis=1, tile...]
    reduce_scatter x8 -> x0, waiting for transfers between devices: 354 us -> none  [the longest x1 121 us: per_device(): lax.psum_scatter(mlp_part + attn_part, 'mp', scatter_dimension=1, tiled=T...]
    psum x1 -> x0, blocking collectives: 146 us -> none  [per_device(): lax.psum((product(context_flat, out_rows), product(active, down_rows)), '...]
    pallas_call x0 -> x5, Pallas kernels: none -> 141 us  [the longest x2 123 us: block_call(): pl.pallas_call(functools.partial(block_kernel, cfg), out_shape=[out, out,...]
    all_to_all x0 -> x6, starting transfers between devices: none -> 57 us  [the longest x2 29.2 us: reduce_rows(): lax.all_to_all(x.reshape(dp, -1, x.shape[1]), 'dp', 0, 0, tiled=True)]
    all_to_all x0 -> x6, waiting for transfers between devices: none -> 54.2 us  [the longest x2 27.7 us: reduce_rows(): lax.all_to_all(x.reshape(dp, -1, x.shape[1]), 'dp', 0, 0, tiled=True)]
    ppermute x0 -> x21, waiting for transfers between devices: none -> 41.5 us  [swap(): return lax.ppermute(x, axis, [(i, i ^ bit) for i in range(size)])]
  transfers between devices with their start and end apart: 12 -> 27, of which waited for: 4 -> 11; matrix products, arithmetic and copies ran while one was open for 31% -> 11% of each run, Pallas kernels for 0% -> 38%
where the time goes in v1:
time: 365 us; the launch traced here: 359 us
  Pallas kernels  141 us (39%)
  waiting for transfers between devices  95.7 us (26%)
  starting transfers between devices  70.8 us (19%)
  other arithmetic  32.8 us (9%)
  local copies, waits for them, and re-layouts  17.4 us (5%)
    pallas_call x2, Pallas kernels, block_call(): pl.pallas_call(functools.partial(block_kernel, cfg), out_shape=[out, out,...  123 us
    ppermute x21, waiting for transfers between devices, swap(): return lax.ppermute(x, axis, [(i, i ^ bit) for i in range(size)])  41.5 us
    all_to_all x2, starting transfers between devices, reduce_rows(): lax.all_to_all(x.reshape(dp, -1, x.shape[1]), 'dp', 0, 0, tiled=True)  29.2 us
    all_to_all x4, starting transfers between devices, gather_rows(): lax.all_to_all(jnp.broadcast_to(x[None], (dp,) + x.shape), 'dp', 0, 0, ti...  27.8 us
    all_to_all x2, waiting for transfers between devices, reduce_rows(): lax.all_to_all(x.reshape(dp, -1, x.shape[1]), 'dp', 0, 0, tiled=True)  27.7 us
    all_to_all x4, waiting for transfers between devices, gather_rows(): lax.all_to_all(jnp.broadcast_to(x[None], (dp,) + x.shape), 'dp', 0, 0, ti...  26.5 us
    another operation x14, other arithmetic, adam_step(): jnp.stack([first_moment * keep_mask, second_moment * keep_mask])  14.2 us
    ppermute x21, starting transfers between devices, swap(): return lax.ppermute(x, axis, [(i, i ^ bit) for i in range(size)])  13.8 us
  transfers between devices with their start and end apart: 27, of which 11 were waited for; matrix products, arithmetic and copies ran while one was open for 11% of the time, Pallas kernels for 38%

profile of v1, /device:TPU:0, one launch (start us, length us, event | category | flops | bytes accessed | tf_op | source)
XLA Modules:
  0.0 359.0 jit_solution(14717930965306007432)
XLA Ops:
  1.3 0.8 convert_element_type.90
  2.0 0.8 convert_element_type.91
  2.8 3.0 collective-permute-start.2
  5.8 2.6 fusion.45
  8.5 0.8 broadcast_in_dim.21
  9.4 5.8 %all-to-all-start = ((bf16[8,16,2048]{2,1,0:T(8,128)(2,1)}), bf16[8,16,2048]{2,1,0:T(8,128)(2,1)}, u32[]{:S(2)}, u32[]{:S(2)}) async-start(bf16[8,16,2048]{2,1,0:T(8,128)(2,1)} %broadcast_in_dim.21), calls=%async_computation | async-start | bytes 1048576 | tf_op jit(solution)/shard_map/all_to_all | solution.py:619
  15.2 1.5 fusion.46
  16.7 1.3 collective-permute-start.3
  18.0 0.8 collective-permute-start.8
  18.8 10.9 %all-to-all-done.refs_18_ = bf16[8,16,2048]{2,1,0:T(8,128)(2,1)} async-done(((bf16[8,16,2048]{2,1,0:T(8,128)(2,1)}), bf16[8,16,2048]{2,1,0:T(8,128)(2,1)}, u32[]{:S(2)}, u32[]{:S(2)}) %all-to-all-start) | async-done | bytes 524320 | tf_op jit(solution)/shard_map/all_to_all | solution.py:619
  29.7 1.0 broadcast_in_dim.22
  30.7 4.2 %all-to-all-start.1 = ((bf16[8,16,3072]{2,1,0:T(8,128)(2,1)}), bf16[8,16,3072]{2,1,0:T(8,128)(2,1)}, u32[]{:S(2)}, u32[]{:S(2)}) async-start(bf16[8,16,3072]{2,1,0:T(8,128)(2,1)} %broadcast_in_dim.22), calls=%async_computation.1 | async-start | bytes 1572864 | tf_op jit(solution)/shard_map/all_to_all | solution.py:619
  34.9 8.3 %collective-permute-done.3.refs_5_ = bf16[2048,256]{1,0:T(8,128)(2,1)} collective-permute-done((bf16[2048,256]{1,0:T(8,128)(2,1)}, bf16[2048,256]{1,0:T(8,128)(2,1)}, u32[]{:S(2)}, u32[]{:S(2)}) %collective-permute-start.3) | collective-permute-done | bytes 1048608 | tf_op jit(solution)/shard_map/ppermute | solution.py:580
  43.2 21.0 %collective-permute-done.8.refs_4_ = bf16[2048,256]{1,0:T(8,128)(2,1)} collective-permute-done((bf16[2048,256]{1,0:T(8,128)(2,1)S(1)}, bf16[2048,256]{1,0:T(8,128)(2,1)}, u32[]{:S(2)}, u32[]{:S(2)}) %collective-permute-start.8) | collective-permute-done | bytes 1048608 | tf_op jit(solution)/shard_map/ppermute | solution.py:580
  64.7 2.0 fusion.6
  67.3 1.1 concatenate.69
  68.4 1.1 concatenate.68
  69.6 1.1 concatenate.67
  71.9 1.2 pad_maximum_fusion.refs_12_
  73.2 0.7 collective-permute-start.6
  73.9 1.4 collective-permute-start.7
  75.9 76.2 %block.2 = (bf16[2,2048,512]{2,1,0:T(8,128)(2,1)}, bf16[2,2048,512]{2,1,0:T(8,128)(2,1)}, f32[128,5120]{1,0:T(8,128)}, f32[256,1024]{1,0:T(8,128)}) custom-call(s32[3]{0:T(128)} %pad_add_fusion.1.scal, bf16[4096,256]{1,0:T(8,128)(2,1)} %refs_3_.4, bf16[4096,256]{1,0:T(8,128)(2,1)} %refs_4_.3, bf16[4096,256]{1,0:T(8,128)(2,1)} %collective-permute-done.refs_2_, ...), custom_call_target="tpu_custom_call" | custom-call | flops 96636764160 | bytes 33554432 | tf_op jit(solution)/shard_map/block/pallas_call | solution.py:435
  153.4 2.1 collective-permute-done.10.refs_6_
  155.5 1.2 collective-permute-done.11.refs_7_
  156.7 46.4 %block.3 = (bf16[2,2048,512]{2,1,0:T(8,128)(2,1)}, bf16[2,2048,512]{2,1,0:T(8,128)(2,1)}, bf16[128,3072]{1,0:T(8,128)(2,1)}, bf16[2,8,16,512]{3,2,1,0:T(8,128)(2...) custom-call(s32[3]{0:T(128)} %pad_add_fusion.scal, ...), custom_call_target="tpu_custom_call" | custom-call | flops 96636764160 | bytes 33554432 | tf_op jit(solution)/shard_map/block/pallas_call | solution.py:435
  203.7 1.2 collective-permute-done.13
  205.0 1.0 convert_add_fusion.1
  206.0 1.0 convert_add_fusion
  207.1 0.7 collective-permute-start.15
  207.8 7.7 %collective-permute-done.15 = bf16[128,1024]{1,0:T(8,128)(2,1)S(1)} collective-permute-done((bf16[128,1024]{1,0:T(8,128)(2,1)S(1)}, bf16[128,1024]{1,0:T(8,128)(2,1)S(1)}, u32[]{:S(2)}, u32[]{:S(2)}) %collective-permute-start.15) | collective-permute-done | bytes 262176 | tf_op jit(solution)/shard_map/ppermute | solution.py:580
  215.5 0.8 fusion.4
  216.3 4.1 %add_convert_fusion = bf16[2,2048,256]{2,1,0:T(8,128)(2,1)} fusion(bf16[2,2048,512]{2,1,0:T(8,128)(2,1)} %collective-permute-done.16.refs_1_, bf16[2,2048,512]{2,1,0:T(8,128)(2,1)} %get-tuple-element.52.refs_0_), kind=kLoop, calls=%fused_computation | loop fusion | flops 4194304 | bytes 6291456 | tf_op jit(solution)/shard_map/convert_element_type | solution.py:763
  220.3 0.7 collective-permute-start.17
  221.0 25.7 %all-to-all-start.2 = ((bf16[8,16,1024]{2,1,0:T(8,128)(2,1)}), bf16[8,16,1024]{2,1,0:T(8,128)(2,1)S(1)}, u32[]{:S(2)}, u32[]{:S(2)}) async-start(bf16[8,16,1024]{2,1,0:T(8,128)(2,1)} %bitcast.20), calls=%async_computation.2 | async-start | bytes 524288 | tf_op jit(solution)/shard_map/all_to_all | solution.py:656
  246.7 8.3 %all-to-all-done.2 = bf16[8,16,1024]{2,1,0:T(8,128)(2,1)S(1)} async-done(((bf16[8,16,1024]{2,1,0:T(8,128)(2,1)}), bf16[8,16,1024]{2,1,0:T(8,128)(2,1)S(1)}, u32[]{:S(2)}, u32[]{:S(2)}) %all-to-all-start.2) | async-done | bytes 262176 | tf_op jit(solution)/shard_map/all_to_all | solution.py:656
  254.9 3.5 all-to-all-start.3
  258.6 19.4 %all-to-all-done.3 = bf16[8,16,3072]{2,1,0:T(8,128)(2,1)S(1)} async-done(((bf16[8,16,3072]{2,1,0:T(8,128)(2,1)}), bf16[8,16,3072]{2,1,0:T(8,128)(2,1)S(1)}, u32[]{:S(2)}, u32[]{:S(2)}) %all-to-all-start.3) | async-done | bytes 786464 | tf_op jit(solution)/shard_map/all_to_all | solution.py:656
  278.4 1.4 fusion.35
  279.8 1.4 collective-permute-start.18
  281.1 0.8 select_bitcast_fusion.5
  282.0 0.7 select_bitcast_fusion.1
  282.6 1.5 select_bitcast_fusion.4
  284.2 1.5 select_bitcast_fusion
  285.7 4.1 %add_convert_fusion.1 = bf16[2,2048,256]{2,1,0:T(8,128)(2,1)} fusion(bf16[2,2048,512]{2,1,0:T(8,128)(2,1)} %collective-permute-done.12.refs_1_, bf16[2,2048,512]{2,1,0:T(8,128)(2,1)} %get-tuple-element.57.refs_0_), kind=kLoop, calls=%fused_computation.1 | loop fusion | flops 4194304 | bytes 6291456 | tf_op jit(solution)/shard_map/convert_element_type | solution.py:763
  289.9 0.7 select_bitcast_fusion.3
  290.5 0.8 broadcast_in_dim.55
  291.4 14.1 %all-to-all-start.5 = ((bf16[8,16,2048]{2,1,0:T(8,128)(2,1)}), bf16[8,16,2048]{2,1,0:T(8,128)(2,1)S(1)}, u32[]{:S(2)}, u32[]{:S(2)}) async-start(bf16[8,16,2048]{2,1,0:T(8,128)(2,1)} %broadcast_in_dim.55), calls=%async_computation.5 | async-start | bytes 1048576 | tf_op jit(solution)/shard_map/all_to_all | solution.py:619
  306.1 0.7 select_bitcast_fusion.2
  306.8 1.4 collective-permute-start.19
  308.8 9.5 %all-to-all-done.5.refs_5_ = bf16[8,16,2048]{2,1,0:T(8,128)(2,1)S(1)} async-done(((bf16[8,16,2048]{2,1,0:T(8,128)(2,1)}), bf16[8,16,2048]{2,1,0:T(8,128)(2,1)S(1)}, u32[]{:S(2)}, u32[]{:S(2)}) %all-to-all-start.5) | async-done | bytes 524320 | tf_op jit(solution)/shard_map/all_to_all | solution.py:619
  318.3 1.0 broadcast_in_dim.54
  319.2 3.7 %all-to-all-start.4 = ((bf16[8,16,3072]{2,1,0:T(8,128)(2,1)}), bf16[8,16,3072]{2,1,0:T(8,128)(2,1)S(1)}, u32[]{:S(2)}, u32[]{:S(2)}) async-start(bf16[8,16,3072]{2,1,0:T(8,128)(2,1)} %broadcast_in_dim.54), calls=%async_computation.4 | async-start | bytes 1572864 | tf_op jit(solution)/shard_map/all_to_all | solution.py:619
  322.9 6.1 %finish.2 = (f32[4096,256]{1,0:T(8,128)}, f32[4096,256]{1,0:T(8,128)}) custom-call(s32[2]{0:T(128)} %copy-done.27, bf16[2,2048,512]{2,1,0:T(8,128)(2,1)} %get-tuple-element.52.refs_0_, bf16[2,2048,512]{2,1,0:T(8,128)(2,1)} %collective-permute-done.16.refs_1_, bf16[2,2048,256]{2,1,0:T(8,128)(2,1)} %copy-done.5, bf16[4096,256]{1,0:T(8,128)(2,1)} %refs_3_.4, ...), custom_call_target="tpu_custom_call" | custom-call | flops 4194304 | bytes 10485760 | tf_op jit(solution)/shard_map/finish/pallas_call | solution.py:498
  329.0 0.6 pad_maximum_fusion.8
  329.8 1.4 pad_maximum_fusion.11
  331.8 1.4 pad_maximum_fusion.5
  333.2 1.5 pad_maximum_fusion.1
  334.8 1.5 pad_maximum_fusion.2
  336.3 6.1 %all-to-all-done.4 = bf16[8,16,3072]{2,1,0:T(8,128)(2,1)S(1)} async-done(((bf16[8,16,3072]{2,1,0:T(8,128)(2,1)}), bf16[8,16,3072]{2,1,0:T(8,128)(2,1)S(1)}, u32[]{:S(2)}, u32[]{:S(2)}) %all-to-all-start.4) | async-done | bytes 786464 | tf_op jit(solution)/shard_map/all_to_all | solution.py:619
  342.4 1.6 copy-done
  344.0 1.6 copy-done.1
  345.6 1.0 copy-done.3
  346.6 6.0 %merge.1 = (f32[1024,768]{1,0:T(8,128)}, f32[1024,1024]{1,0:T(8,128)}, f32[1024,1024]{1,0:T(8,128)}, f32[256,1024]{1,0:T(8,128)}) custom-call(s32[1]{0:T(128)} %bitcast.scal, bf16[1024,768]{1,0:T(8,128)(2,1)S(1)} %copy-done.2, bf16[1024,1024]{1,0:T(8,128)(2,1)S(1)} %copy-done, bf16[1024,1024]{1,0:T(8,128)(2,1)S(1)} %copy-done.1, ...), custom_call_target="tpu_custom_call" | custom-call | flops 805306368 | bytes 20971520 | tf_op jit(solution)/shard_map/merge/pallas_call | solution.py:551
  352.6 6.0 %finish.3 = (f32[4096,256]{1,0:T(8,128)}, f32[4096,256]{1,0:T(8,128)}) custom-call(s32[2]{0:T(128)} %copy-done.28, bf16[2,2048,512]{2,1,0:T(8,128)(2,1)} %get-tuple-element.57.refs_0_, bf16[2,2048,512]{2,1,0:T(8,128)(2,1)} %collective-permute-done.12.refs_1_, ...), custom_call_target="tpu_custom_call", output_to_operand_aliasing={{0}: (7, {}), {1}: (8, {})} | custom-call | flops 4194304 | bytes 10485760 | tf_op jit(solution)/shard_map/finish/pallas_call | solution.py:498
  (135 shorter events, 8.0 us)
Async XLA Ops:
  0.7 74.6 %collective-permute-start = (bf16[4096,256]{1,0:T(8,128)(2,1)}, bf16[4096,256]{1,0:T(8,128)(2,1)}, u32[]{:S(2)}, u32[]{:S(2)}) collective-permute-start(bf16[4096,256]{1,0:T(8,128)(2,1)} %refs_3_.4), channel_id=1, source_target_pairs={{0,1},{1,0},{2,3},{3,2},{4,5},{5,4},{6,7},{7,6},{8,9},{9,8},{10,11... | collective-permute-start | bytes 6291464 | tf_op jit(solution)/shard_map/ppermute | solution.py:580
  1.2 74.1 %collective-permute-start.1 = (bf16[4096,256]{1,0:T(8,128)(2,1)}, bf16[4096,256]{1,0:T(8,128)(2,1)}, u32[]{:S(2)}, u32[]{:S(2)}) collective-permute-start(bf16[4096,256]{1,0:T(8,128)(2,1)} %refs_4_.3), channel_id=1, source_target_pairs={{0,1},{1,0},{2,3},{3,2},{4,5},{5,4},{6,7},{7,6},{8,9},{9,8},{10,11... | collective-permute-start | bytes 6291464 | tf_op jit(solution)/shard_map/ppermute | solution.py:580
  2.8 12.3 %copy-start.4 = (bf16[4096,256]{1,0:T(8,128)(2,1)S(1)}, bf16[4096,256]{1,0:T(8,128)(2,1)}, u32[]{:S(2)}) copy-start(bf16[4096,256]{1,0:T(8,128)(2,1)} %refs_4_.3) | copy-start | bytes 6291460
  2.8 5.7 %collective-permute-start.2 = (bf16[16,1024]{1,0:T(8,128)(2,1)S(1)}, bf16[16,1024]{1,0:T(8,128)(2,1)S(1)}, u32[]{:S(2)}, u32[]{:S(2)}) collective-permute-start(bf16[16,1024]{1,0:T(8,128)(2,1)S(1)} %constant_dynamic-update-slice_fusion), channel_id=1, source_target_pairs={{0,2},{1,3},{2,0},{3,1},{4,6},{5,7},{6,4},{7,5},{8,10},{9,11},{10,... | collective-permute-start | bytes 98312 | tf_op jit(solution)/shard_map/ppermute | solution.py:580
  9.4 20.4 %all-to-all-start = ((bf16[8,16,2048]{2,1,0:T(8,128)(2,1)}), bf16[8,16,2048]{2,1,0:T(8,128)(2,1)}, u32[]{:S(2)}, u32[]{:S(2)}) async-start(bf16[8,16,2048]{2,1,0:T(8,128)(2,1)} %broadcast_in_dim.21), calls=%async_computation | async-start | bytes 1048576 | tf_op jit(solution)/shard_map/all_to_all | solution.py:619
  15.2 1.5 copy-start.15
  15.2 1.5 copy-start.19
  15.2 3.6 %copy-start.24 = (f32[256,16]{0,1:T(8,128)S(1)}, f32[256,16]{0,1:T(8,128)}, u32[]{:S(2)}) copy-start(f32[256,16]{0,1:T(8,128)} %param.39) | copy-start | bytes 49156
  15.2 3.6 %copy-start.14 = (f32[1024,16]{0,1:T(8,128)S(1)}, f32[1024,16]{0,1:T(8,128)}, u32[]{:S(2)}) copy-start(f32[1024,16]{0,1:T(8,128)} %param.40) | copy-start | bytes 196612
  16.7 26.5 %collective-permute-start.3 = (bf16[2048,256]{1,0:T(8,128)(2,1)}, bf16[2048,256]{1,0:T(8,128)(2,1)}, u32[]{:S(2)}, u32[]{:S(2)}) collective-permute-start(bf16[2048,256]{1,0:T(8,128)(2,1)} %get-tuple-element.48), channel_id=1, source_target_pairs={{0,2},{1,3},{2,0},{3,1},{4,6},{5,7},{6,4},{7,5},{8,10},{9,11},{10,... | collective-permute-start | bytes 3145736 | tf_op jit(solution)/shard_map/ppermute | solution.py:580
  18.0 46.1 %collective-permute-start.8 = (bf16[2048,256]{1,0:T(8,128)(2,1)S(1)}, bf16[2048,256]{1,0:T(8,128)(2,1)}, u32[]{:S(2)}, u32[]{:S(2)}) collective-permute-start(bf16[2048,256]{1,0:T(8,128)(2,1)S(1)} %get-tuple-element.51), channel_id=1, source_target_pairs={{0,2},{1,3},{2,0},{3,1},{4,6},{5,7},{6,4},{7,5},{8,10},{9,11},{10,... | collective-permute-start | bytes 3145736 | tf_op jit(solution)/shard_map/ppermute | solution.py:580
  18.8 47.8 %copy-start.26 = (f32[768]{0:T(1024)S(1)}, f32[768]{0:T(1024)}, u32[]{:S(2)}) copy-start(f32[768]{0:T(1024)} %param.33) | copy-start | bytes 9220
  30.7 42.5 %all-to-all-start.1 = ((bf16[8,16,3072]{2,1,0:T(8,128)(2,1)}), bf16[8,16,3072]{2,1,0:T(8,128)(2,1)}, u32[]{:S(2)}, u32[]{:S(2)}) async-start(bf16[8,16,3072]{2,1,0:T(8,128)(2,1)} %broadcast_in_dim.22), calls=%async_computation.1 | async-start | bytes 1572864 | tf_op jit(solution)/shard_map/all_to_all | solution.py:619
  43.2 30.0 %collective-permute-start.4 = (bf16[2048,256]{1,0:T(8,128)(2,1)}, bf16[2048,256]{1,0:T(8,128)(2,1)}, u32[]{:S(2)}, u32[]{:S(2)}) collective-permute-start(bf16[2048,256]{1,0:T(8,128)(2,1)} %collective-permute-done.3.refs_5_), channel_id=1, source_target_pairs={{0,1},{1,0},{2,3},{3,2},{4,5},{5,4},{6,7},{7,6},{8,9},{9,8},{10,11... | collective-permute-start | bytes 3145736 | tf_op jit(solution)/shard_map/ppermute | solution.py:580
  64.1 11.2 %collective-permute-start.9 = (bf16[2048,256]{1,0:T(8,128)(2,1)}, bf16[2048,256]{1,0:T(8,128)(2,1)}, u32[]{:S(2)}, u32[]{:S(2)}) collective-permute-start(bf16[2048,256]{1,0:T(8,128)(2,1)} %collective-permute-done.8.refs_4_), channel_id=1, source_target_pairs={{0,1},{1,0},{2,3},{3,2},{4,5},{5,4},{6,7},{7,6},{8,9},{9,8},{10,11... | collective-permute-start | bytes 3145736 | tf_op jit(solution)/shard_map/ppermute | solution.py:580
  64.2 9.0 %collective-permute-start.5 = (bf16[128,2048]{1,0:T(8,128)(2,1)}, bf16[128,2048]{1,0:T(8,128)(2,1)}, u32[]{:S(2)}, u32[]{:S(2)}) collective-permute-start(bf16[128,2048]{1,0:T(8,128)(2,1)} %bitcast.7.refs_20_), channel_id=1, source_target_pairs={{0,1},{1,0},{2,3},{3,2},{4,5},{5,4},{6,7},{7,6},{8,9},{9,8},{10,11... | collective-permute-start | bytes 1572872 | tf_op jit(solution)/shard_map/ppermute | solution.py:580
  69.6 1.2 copy-start.29
  70.7 2.4 copy-start.6
  70.8 0.5 copy-start.27
  70.8 81.9 %copy-start.28 = (s32[2]{0:T(128)}, s32[2]{0:T(128)S(1)}, u32[]{:S(2)}) copy-start(s32[2]{0:T(128)S(1)} %get-tuple-element.120.lens) | copy-start | bytes 28
  73.2 78.9 %collective-permute-start.6 = (bf16[2048,256]{1,0:T(8,128)(2,1)S(1)}, bf16[2048,256]{1,0:T(8,128)(2,1)S(1)}, u32[]{:S(2)}, u32[]{:S(2)}) collective-permute-start(bf16[2048,256]{1,0:T(8,128)(2,1)S(1)} %copy-done.6), channel_id=1, source_target_pairs={{0,2},{1,3},{2,0},{3,1},{4,6},{5,7},{6,4},{7,5},{8,10},{9,11},{10,... | collective-permute-start | bytes 3145736 | tf_op jit(solution)/shard_map/ppermute | solution.py:580
  73.9 78.3 %collective-permute-start.7 = (bf16[2048,256]{1,0:T(8,128)(2,1)}, bf16[2048,256]{1,0:T(8,128)(2,1)}, u32[]{:S(2)}, u32[]{:S(2)}) collective-permute-start(bf16[2048,256]{1,0:T(8,128)(2,1)} %get-tuple-element.50), channel_id=1, source_target_pairs={{0,2},{1,3},{2,0},{3,1},{4,6},{5,7},{6,4},{7,5},{8,10},{9,11},{10,... | collective-permute-start | bytes 3145736 | tf_op jit(solution)/shard_map/ppermute | solution.py:580
  152.1 4.6 %copy-start.30 = (bf16[2048,256]{1,0:T(8,128)(2,1)}, bf16[2048,256]{1,0:T(8,128)(2,1)S(1)}, u32[]{:S(2)}) copy-start(bf16[2048,256]{1,0:T(8,128)(2,1)S(1)} %collective-permute-done.6.refs_4_) | copy-start | bytes 3145732
  152.1 3.3 collective-permute-start.10
  152.2 4.5 %collective-permute-start.11 = (bf16[2048,256]{1,0:T(8,128)(2,1)}, bf16[2048,256]{1,0:T(8,128)(2,1)}, u32[]{:S(2)}, u32[]{:S(2)}) collective-permute-start(bf16[2048,256]{1,0:T(8,128)(2,1)} %collective-permute-done.7.refs_5_), channel_id=1, source_target_pairs={{0,1},{1,0},{2,3},{3,2},{4,5},{5,4},{6,7},{7,6},{8,9},{9,8},{10,11... | collective-permute-start | bytes 3145736 | tf_op jit(solution)/shard_map/ppermute | solution.py:580
  153.3 63.0 %collective-permute-start.16 = (bf16[2,2048,512]{2,1,0:T(8,128)(2,1)}, bf16[2,2048,512]{2,1,0:T(8,128)(2,1)}, u32[]{:S(2)}, u32[]{:S(2)}) collective-permute-start(bf16[2,2048,512]{2,1,0:T(8,128)(2,1)} %get-tuple-element.64), channel_id=1, source_target_pairs={{0,1},{1,0},{2,3},{3,2},{4,5},{5,4},{6,7},{7,6},{8,9},{9,8},{10,11... | collective-permute-start | bytes 12582920 | tf_op jit(solution)/shard_map/ppermute | solution.py:580
  155.5 1.2 copy-start.31
  203.1 1.8 collective-permute-start.13
  203.4 2.6 collective-permute-start.14
  207.1 8.4 %collective-permute-start.15 = (bf16[128,1024]{1,0:T(8,128)(2,1)S(1)}, bf16[128,1024]{1,0:T(8,128)(2,1)S(1)}, u32[]{:S(2)}, u32[]{:S(2)}) collective-permute-start(bf16[128,1024]{1,0:T(8,128)(2,1)S(1)} %fusion.7), channel_id=1, source_target_pairs={{0,2},{1,3},{2,0},{3,1},{4,6},{5,7},{6,4},{7,5},{8,10},{9,11},{10,... | collective-permute-start | bytes 786440 | tf_op jit(solution)/shard_map/ppermute | solution.py:580
  220.3 57.9 %copy-start.10 = (f32[2,2,32,128]{3,2,1,0:T(8,128)S(1)}, f32[2,2,32,128]{3,2,1,0:T(8,128)}, u32[]{:S(2)}) copy-start(f32[2,2,32,128]{3,2,1,0:T(8,128)} %param.42) | copy-start | bytes 196612
  220.3 57.9 %copy-start.21 = (f32[2,32,128]{2,1,0:T(8,128)S(1)}, f32[2,32,128]{2,1,0:T(8,128)}, u32[]{:S(2)}) copy-start(f32[2,32,128]{2,1,0:T(8,128)} %param.36) | copy-start | bytes 98308
  220.3 58.0 %copy-start.17 = (f32[2,2,16,256]{3,2,1,0:T(8,128)S(1)}, f32[2,2,16,256]{3,2,1,0:T(8,128)}, u32[]{:S(2)}) copy-start(f32[2,2,16,256]{3,2,1,0:T(8,128)} %param.47) | copy-start | bytes 196612
  220.3 57.8 %collective-permute-start.17 = (bf16[2,2048,256]{2,1,0:T(8,128)(2,1)}, bf16[2,2048,256]{2,1,0:T(8,128)(2,1)S(1)}, u32[]{:S(2)}, u32[]{:S(2)}) collective-permute-start(bf16[2,2048,256]{2,1,0:T(8,128)(2,1)} %add_convert_fusion), channel_id=1, source_target_pairs={{0,2},{1,3},{2,0},{3,1},{4,6},{5,7},{6,4},{7,5},{8,10},{9,11},{10,... | collective-permute-start | bytes 6291464 | tf_op jit(solution)/shard_map/ppermute | solution.py:580
  221.0 61.0 %copy-start.8 = (f32[2,1024,16]{1,2,0:T(8,128)S(1)}, f32[2,1024,16]{1,2,0:T(8,128)}, u32[]{:S(2)}) copy-start(f32[2,1024,16]{1,2,0:T(8,128)} %param.46) | copy-start | bytes 393220
  221.0 33.9 %all-to-all-start.2 = ((bf16[8,16,1024]{2,1,0:T(8,128)(2,1)}), bf16[8,16,1024]{2,1,0:T(8,128)(2,1)S(1)}, u32[]{:S(2)}, u32[]{:S(2)}) async-start(bf16[8,16,1024]{2,1,0:T(8,128)(2,1)} %bitcast.20), calls=%async_computation.2 | async-start | bytes 524288 | tf_op jit(solution)/shard_map/all_to_all | solution.py:656
  254.9 23.1 %all-to-all-start.3 = ((bf16[8,16,3072]{2,1,0:T(8,128)(2,1)}), bf16[8,16,3072]{2,1,0:T(8,128)(2,1)S(1)}, u32[]{:S(2)}, u32[]{:S(2)}) async-start(bf16[8,16,3072]{2,1,0:T(8,128)(2,1)} %bitcast.211), calls=%async_computation.3 | async-start | bytes 1572864 | tf_op jit(solution)/shard_map/all_to_all | solution.py:656
  258.5 27.2 %collective-permute-start.12 = (bf16[2,2048,512]{2,1,0:T(8,128)(2,1)}, bf16[2,2048,512]{2,1,0:T(8,128)(2,1)}, u32[]{:S(2)}, u32[]{:S(2)}) collective-permute-start(bf16[2,2048,512]{2,1,0:T(8,128)(2,1)} %get-tuple-element.58), channel_id=1, source_target_pairs={{0,1},{1,0},{2,3},{3,2},{4,5},{5,4},{6,7},{7,6},{8,9},{9,8},{10,11... | collective-permute-start | bytes 12582920 | tf_op jit(solution)/shard_map/ppermute | solution.py:580
  278.2 11.6 %copy-start.5 = (bf16[2,2048,256]{2,1,0:T(8,128)(2,1)}, bf16[2,2048,256]{2,1,0:T(8,128)(2,1)S(1)}, u32[]{:S(2)}) copy-start(bf16[2,2048,256]{2,1,0:T(8,128)(2,1)S(1)} %collective-permute-done.17.refs_2_) | copy-start | bytes 6291460
  278.2 50.8 %copy-start.7 = (f32[16,2,2,128]{3,0,2,1:T(8,128)}, f32[16,2,2,128]{3,0,2,1:T(8,128)S(1)}, u32[]{:S(2)}) copy-start(f32[16,2,2,128]{3,0,2,1:T(8,128)S(1)} %copy.44) | copy-start | bytes 98308
  279.8 10.7 %collective-permute-start.18 = (bf16[16,1024]{1,0:T(8,128)(2,1)S(1)}, bf16[16,1024]{1,0:T(8,128)(2,1)S(1)}, u32[]{:S(2)}, u32[]{:S(2)}) collective-permute-start(bf16[16,1024]{1,0:T(8,128)(2,1)S(1)} %constant_dynamic-update-slice_fusion.6), channel_id=1, source_target_pairs={{0,2},{1,3},{2,0},{3,1},{4,6},{5,7},{6,4},{7,5},{8,10},{9,11},{10,... | collective-permute-start | bytes 98312 | tf_op jit(solution)/shard_map/ppermute | solution.py:580
  282.0 7.8 %copy-start.20 = (f32[16,768]{1,0:T(8,128)}, f32[16,768]{1,0:T(8,128)S(1)}, u32[]{:S(2)}) copy-start(f32[16,768]{1,0:T(8,128)S(1)} %get-tuple-element.91) | copy-start | bytes 147460
  282.6 7.2 %copy-start.11 = (f32[1024,16]{0,1:T(8,128)}, f32[1024,16]{0,1:T(8,128)S(1)}, u32[]{:S(2)}) copy-start(f32[1024,16]{0,1:T(8,128)S(1)} %get-tuple-element.82) | copy-start | bytes 196612
  285.7 4.1 %copy-start.9 = (f32[2,16,1024]{2,1,0:T(8,128)S(1)}, f32[2,16,1024]{2,1,0:T(8,128)}, u32[]{:S(2)}) copy-start(f32[2,16,1024]{2,1,0:T(8,128)} %param.44) | copy-start | bytes 393220
  289.8 15.6 %copy-start.22 = (f32[2,256,16]{1,2,0:T(8,128)S(1)}, f32[2,256,16]{1,2,0:T(8,128)}, u32[]{:S(2)}) copy-start(f32[2,256,16]{1,2,0:T(8,128)} %param.45) | copy-start | bytes 98308
  289.8 16.3 %copy-start.16 = (f32[16,1024]{1,0:T(8,128)S(1)}, f32[16,1024]{1,0:T(8,128)}, u32[]{:S(2)}) copy-start(f32[16,1024]{1,0:T(8,128)} %param.38) | copy-start | bytes 196612
  289.8 18.3 %copy-start.25 = (f32[256,16]{0,1:T(8,128)S(1)}, f32[256,16]{0,1:T(8,128)}, u32[]{:S(2)}) copy-start(f32[256,16]{0,1:T(8,128)} %param.39) | copy-start | bytes 49156
  290.5 28.7 %copy-start.12 = (f32[16,1024]{1,0:T(8,128)}, f32[16,1024]{1,0:T(8,128)S(1)}, u32[]{:S(2)}) copy-start(f32[16,1024]{1,0:T(8,128)S(1)} %get-tuple-element.88) | copy-start | bytes 196612
  291.4 26.9 %all-to-all-start.5 = ((bf16[8,16,2048]{2,1,0:T(8,128)(2,1)}), bf16[8,16,2048]{2,1,0:T(8,128)(2,1)S(1)}, u32[]{:S(2)}, u32[]{:S(2)}) async-start(bf16[8,16,2048]{2,1,0:T(8,128)(2,1)} %broadcast_in_dim.55), calls=%async_computation.5 | async-start | bytes 1048576 | tf_op jit(solution)/shard_map/all_to_all | solution.py:619
  306.1 16.8 %copy-start.23 = (f32[256,16]{0,1:T(8,128)}, f32[256,16]{0,1:T(8,128)S(1)}, u32[]{:S(2)}) copy-start(f32[256,16]{0,1:T(8,128)S(1)} %get-tuple-element.85) | copy-start | bytes 49156
  306.8 45.8 %collective-permute-start.19 = (bf16[2,2048,256]{2,1,0:T(8,128)(2,1)}, bf16[2,2048,256]{2,1,0:T(8,128)(2,1)}, u32[]{:S(2)}, u32[]{:S(2)}) collective-permute-start(bf16[2,2048,256]{2,1,0:T(8,128)(2,1)} %add_convert_fusion.1), channel_id=1, source_target_pairs={{0,2},{1,3},{2,0},{3,1},{4,6},{5,7},{6,4},{7,5},{8,10},{9,11},{10,... | collective-permute-start | bytes 6291464 | tf_op jit(solution)/shard_map/ppermute | solution.py:580
  319.2 23.1 %all-to-all-start.4 = ((bf16[8,16,3072]{2,1,0:T(8,128)(2,1)}), bf16[8,16,3072]{2,1,0:T(8,128)(2,1)S(1)}, u32[]{:S(2)}, u32[]{:S(2)}) async-start(bf16[8,16,3072]{2,1,0:T(8,128)(2,1)} %broadcast_in_dim.54), calls=%async_computation.4 | async-start | bytes 1572864 | tf_op jit(solution)/shard_map/all_to_all | solution.py:619
  322.9 6.8 %copy-start.18 = (f32[2,2,16,256]{3,2,1,0:T(8,128)S(1)}, f32[2,2,16,256]{3,2,1,0:T(8,128)}, u32[]{:S(2)}) copy-start(f32[2,2,16,256]{3,2,1,0:T(8,128)} %param.47) | copy-start | bytes 196612
  322.9 11.8 %copy-start.13 = (f32[1,1024,16]{1,2,0:T(8,128)S(1)}, f32[1,1024,16]{1,2,0:T(8,128)}, u32[]{:S(2)}) copy-start(f32[1,1024,16]{1,2,0:T(8,128)} %get-tuple-element.80) | copy-start | bytes 196612
  322.9 19.4 %copy-start.2 = (bf16[1024,768]{1,0:T(8,128)(2,1)S(1)}, bf16[1024,768]{1,0:T(8,128)(2,1)}, u32[]{:S(2)}) copy-start(bf16[1024,768]{1,0:T(8,128)(2,1)} %refs_0_.5) | copy-start | bytes 4718596
  329.7 12.7 %collective-permute-start.20 = (bf16[128,2048]{1,0:T(8,128)(2,1)S(1)}, bf16[128,2048]{1,0:T(8,128)(2,1)S(1)}, u32[]{:S(2)}, u32[]{:S(2)}) collective-permute-start(bf16[128,2048]{1,0:T(8,128)(2,1)S(1)} %bitcast.202), channel_id=1, source_target_pairs={{0,1},{1,0},{2,3},{3,2},{4,5},{5,4},{6,7},{7,6},{8,9},{9,8},{10,11... | collective-permute-start | bytes 1572872 | tf_op jit(solution)/shard_map/ppermute | solution.py:580
  342.4 1.6 copy-start
  344.0 1.6 copy-start.1
  345.6 1.0 copy-start.3

commit v2 on v1

--- a/solution.py
+++ b/solution.py
@@ -3,6 +3,7 @@
 
 import jax
 import jax.numpy as jnp
+import numpy as np
 from jax import lax
 from jax.experimental import pallas as pl
 from jax.experimental.pallas import tpu as pltpu
@@ -77,7 +78,8 @@
     received, refs = refs[: 2 * parts - 4], refs[2 * parts - 4 :]
     (gain, shift, b_qkv, b_up, rope, w_qkv, w_up, w_down, w_out, f_split), refs = refs[:10], refs[10:]
     sources, refs = refs[:n_src], refs[n_src:]
-    (acc_in, res_in, keep, send), refs = refs[:4], refs[4:]
+    (acc_in, res_in), refs = refs[:2], refs[2:]
+    outs, refs = refs[: 2 * parts], refs[2 * parts :]
     sums, refs = refs[: len(refs) - 31], refs[len(refs) - 31 :]
     (
         fin_v, gin_b, gres_b, gsplit_b, x_v, c_v, wq_v, wu_v, wd_v, ft_v, rope_v, acc_v, res_v,
@@ -89,6 +91,7 @@
     steps = length // tile
     mixed_cols = 3 * wide
     joint = units + wide
+    skip = f_split.shape[1] - mixed_cols - units - joint
 
     def tiles_of(s):
         return (scal[s] + tile - 1) // tile
@@ -105,7 +108,7 @@
                 at = pl.ds(pl.multiple_of(s * length + t * tile, tile), tile)
                 if k < 2:
                     src = whole_rows[2 * k + which].at[
-                        pl.ds(pl.multiple_of((chunk * seqs + s) * length + t * tile, tile), tile), :
+                        pl.ds(pl.multiple_of((chunk + s) * length + t * tile, tile), tile), :
                     ]
                 else:
                     src = received[2 * (k - 2) + which].at[at, :]
@@ -130,13 +133,11 @@
         for which in range(2):
             for k in range(parts):
                 place = pl.ds(pl.multiple_of(jnp.bitwise_xor(me, k) * cols, cols), cols)
-                target = keep if k % 2 == 0 else send
-                at = (k // 2) * cols
                 rows = pl.ds(pl.multiple_of(s * length + t * tile, tile), tile)
                 found.append(
                     pltpu.make_async_copy(
                         out_v.at[which, row_slice(t), place],
-                        target.at[which, rows, at : at + cols],
+                        outs[2 * k + which].at[rows, :],
                         out_sems.at[t, which * parts + k],
                     )
                 )
@@ -153,13 +154,13 @@
     res_places = (wd_v.at[joint + rank :, :dim], wd_v.at[joint : joint + rank, :dim])
     pairs = [
         (w_qkv, wq_v.at[:dim, :mixed_cols]),
-        (f_split.at[:, :mixed_cols], wq_v.at[dim:, :mixed_cols]),
+        (f_split.at[:, skip : skip + mixed_cols], wq_v.at[dim:, :mixed_cols]),
         (rope, rope_v),
         (w_up, wu_v.at[:dim, :units]),
-        (f_split.at[:, mixed_cols : mixed_cols + units], wu_v.at[dim:, :units]),
+        (f_split.at[:, skip + mixed_cols : skip + mixed_cols + units], wu_v.at[dim:, :units]),
         (w_down, wd_v.at[:units, :dim]),
         (w_out, wd_v.at[units:joint, :dim]),
-        (f_split.at[:, mixed_cols + units :], ft_v),
+        (f_split.at[:, skip + mixed_cols + units :], ft_v),
     ] + input_pairs(sizes, core, sources, fin_v, res_places)
     loads = [pltpu.make_async_copy(a, b, w_sems.at[i]) for i, (a, b) in enumerate(pairs)]
     start_rows(0)
@@ -419,7 +420,7 @@
     operands = [scal, *whole_rows, *received, gain, shift, b_qkv, b_up, rope, *weights, f_split, *sources, *acc]
     specs = [pl.BlockSpec(memory_space=pltpu.SMEM)] + [ANY] * (2 * parts) + [VM] * 4 + [ANY] * (8 + len(sources))
     flops = 2 * seqs * length * (dim * (units * 4 + wide * 8 + rank * 12) + units * rank * 6 + length * wide * 12)
-    out = jax.ShapeDtypeStruct((2, seqs * length, dim // 2), BF)
+    out = [jax.ShapeDtypeStruct((seqs * length, cols), BF)] * (2 * parts)
     if not last:
         sums = [acc_shape, res_shape]
     else:
@@ -434,9 +435,9 @@
     flat = lambda n, dtype: pltpu.VMEM((n, length), dtype)
     return pl.pallas_call(
         functools.partial(block_kernel, cfg),
-        out_shape=[out, out, *sums],
+        out_shape=[*out, *sums],
         in_specs=specs,
-        out_specs=[ANY] * (2 + len(sums)),
+        out_specs=[ANY] * (2 * parts + len(sums)),
         scratch_shapes=[
             pltpu.VMEM(in_shape, BF),
             pltpu.VMEM(in_shape if last else (2, 1, 16, rank), BF),
@@ -462,7 +463,7 @@
             pltpu.SemaphoreType.DMA((steps, 2 * parts)),
             pltpu.SemaphoreType.DMA((5 + 4 * high * (folds + 1),)),
         ],
-        input_output_aliases={} if first or last else {len(operands) - 2: 2, len(operands) - 1: 3},
+        input_output_aliases={} if first or last else {len(operands) - 2: 2 * parts, len(operands) - 1: 2 * parts + 1},
         compiler_params=pltpu.CompilerParams(vmem_limit_bytes=60 * 1024 * 1024),
         cost_estimate=pl.CostEstimate(
             flops=2 * flops, bytes_accessed=32 * 1024 * 1024, transcendentals=2 * seqs * length * units
@@ -480,17 +481,17 @@
     seq_len = lens[at // length]
     position = at % length + lax.broadcasted_iota(jnp.int32, (block, 1), 0)
     valid = position < seq_len
-    total = sum(part[...].astype(F32) for part in parts)
+    total = [sum(part[...].astype(F32) for part in parts[w::2]) for w in range(2)]
     result[...] = jnp.where(valid, tokens[...].astype(F32) + total[0] + bias[0:1, :] + bias[1:2, :], 0.0)
     grad[...] = jnp.where(valid, cotangent[...].astype(F32) + total[1], 0.0)
 
 
 def finish_call(chunk, lens, parts, tokens, cotangent, bias, length, earlier):
     rows, cols = tokens.shape
-    span = parts[0].shape[1]
+    span = parts[0].shape[0]
     block = min(512, length)
-    base = chunk * span // block
-    part_spec = pl.BlockSpec((2, block, cols), lambda i: (0, i, 0))
+    base = chunk * length // block
+    part_spec = pl.BlockSpec((block, cols), lambda i: (i, 0))
     row_spec = pl.BlockSpec((block, cols), lambda i: (base + i, 0))
     specs = [pl.BlockSpec(memory_space=pltpu.SMEM)] + [part_spec] * len(parts) + [row_spec] * 2
     specs += [pl.BlockSpec(bias.shape, lambda i: (0, 0))] + [pl.BlockSpec(memory_space=pl.ANY)] * len(earlier)
@@ -514,7 +515,8 @@
     outs, refs = refs[:4], refs[4:]
     weights_v, outs_v, (fin_v, res0_v, res1_v, split_v, t_v, in_sems, out_sems) = refs[:4], refs[4:8], refs[8:]
     core = lax.rem(scal[0], 2)
-    pairs = input_pairs(sizes, core, sources, fin_v, (res0_v, res1_v)) + [(f_split, split_v)]
+    skip = f_split.shape[1] - split_v.shape[1]
+    pairs = input_pairs(sizes, core, sources, fin_v, (res0_v, res1_v)) + [(f_split.at[:, skip:], split_v)]
     pairs += list(zip((w_qkv, w_up, w_down, w_out), weights_v))
     loads = [pltpu.make_async_copy(a, b, in_sems.at[i]) for i, (a, b) in enumerate(pairs)]
     for load in loads:
@@ -559,7 +561,7 @@
             pltpu.VMEM((2, dp, dim // dp, rank), BF),
             pltpu.VMEM((rank, dim), BF),
             pltpu.VMEM((rank, dim), BF),
-            pltpu.VMEM(f_split.shape, BF),
+            pltpu.VMEM((rank, 4 * wide + 2 * units), BF),
             pltpu.VMEM((units + wide, rank), BF),
             pltpu.SemaphoreType.DMA((5 + (4 * high * (folds + 1) if direct else 3),)),
             pltpu.SemaphoreType.DMA((chunks,)),
@@ -620,18 +622,19 @@
     return found.reshape(dp * x.shape[0], x.shape[1])
 
 
-def gather_inputs(both, sizes, dim, dp, mp):
+def gather_factors(both, split, sizes, dim, dp, mp):
     high, folds, ranks, rank, own_cols, direct = sizes
-    found = gather_rows(both, dp)
-    other = swap(found, "mp", mp, 1)
+    found = gather_rows(jnp.concatenate([both, split], 1), dp)
+    mine = found[:, : both.shape[1]]
+    other = swap(mine, "mp", mp, 1)
     if direct:
         deep = lambda x: x.reshape(dp, ranks, x.shape[1])
-        return [deep(found), deep(other), found, other]
-    cores = jnp.stack(in_order(found, other, "mp", 1)).reshape(2, dp, ranks, high, both.shape[1] // high)
+        return found, [deep(found), deep(other), found, other]
+    cores = jnp.stack(in_order(mine, other, "mp", 1)).reshape(2, dp, ranks, high, both.shape[1] // high)
     in_part = cores[..., : 2 * folds * rank].reshape(2, dp, ranks, high, 2, folds, rank)
     res_part = cores[..., 2 * folds * rank :].reshape(2, dp, ranks, high, 2, own_cols)
     whole_in = in_part.transpose(4, 1, 3, 0, 5, 2, 6).reshape(2, dp, dim // dp, rank)
-    return [whole_in, res_part.transpose(4, 1, 2, 3, 0, 5).reshape(2, rank, dim)]
+    return found, [whole_in, res_part.transpose(4, 1, 2, 3, 0, 5).reshape(2, rank, dim)]
 
 
 def reduce_inputs(sums, sizes, dim, dp, mp):
@@ -668,17 +671,17 @@
 
 def rope_tables(length):
     half = ROT // 2
-    frequency = 10000.0 ** (-jnp.arange(half, dtype=F32) * 2.0 / ROT)
-    angles = jnp.arange(length, dtype=F32)[:, None] * frequency[None, :]
-    cos, sin = jnp.cos(angles), jnp.sin(angles)
-    ones, zeros = jnp.ones((length, HEAD - ROT), F32), jnp.zeros((length, HEAD - ROT), F32)
-    blank = jnp.zeros_like(sin)
+    frequency = 10000.0 ** (-np.arange(half) * 2.0 / ROT)
+    angles = np.arange(length)[:, None] * frequency[None, :]
+    cos, sin = np.cos(angles), np.sin(angles)
+    ones, zeros = np.ones((length, HEAD - ROT)), np.zeros((length, HEAD - ROT))
+    blank = np.zeros_like(sin)
     one_head = [
-        jnp.concatenate([cos, cos, ones], 1),
-        jnp.concatenate([-sin, blank, zeros], 1),
-        jnp.concatenate([blank, sin, zeros], 1),
+        np.concatenate([cos, cos, ones], 1),
+        np.concatenate([-sin, blank, zeros], 1),
+        np.concatenate([blank, sin, zeros], 1),
     ]
-    return jnp.stack([jnp.concatenate([table, table], 1) for table in one_head])
+    return jnp.asarray(np.stack([np.concatenate([t, t], 1) for t in one_head]).astype(np.float32))
 
 
 def per_device(
@@ -716,9 +719,8 @@
     dim, units = up_weight.shape
     me = lax.axis_index("mp").astype(jnp.int32)
     mp_bits = bits_of(mp)
-    seqs = 2 if seq_count % 2 == 0 else 1
-    chunks = seq_count // seqs
-    span = seqs * length
+    plan = [(0, 2), (2, seq_count - 2)]
+    chunks = len(plan)
 
     rank = in_factor.shape[2]
     low = lambda f: f.astype(BF)
@@ -727,12 +729,14 @@
     own_ranks, own_cols = res_factor.shape[1:]
     sizes = (mp // 2, in_factor.shape[1] // own_ranks, own_ranks, rank, own_cols, own_ranks % 16 == 0)
     rank_rows = lambda qkv, up, down, out: jnp.concatenate([low(qkv), low(up), low(down).T, low(out).T], 1)
-    f_split = gather_rows(rank_rows(qkv_factor, up_factor, down_factor, out_factor), dp)
-    sources = gather_inputs(both, sizes, dim, dp, mp)
+    f_split, sources = gather_factors(
+        both, rank_rows(qkv_factor, up_factor, down_factor, out_factor), sizes, dim, dp, mp
+    )
     whole_rows = (tokens, cotangent, swap(tokens, "mp", mp, 1), swap(cotangent, "mp", mp, 1))
 
     def far_rows(c, wait):
-        held = {0: [tokens[c * span : (c + 1) * span], cotangent[c * span : (c + 1) * span]]}
+        rows = slice(plan[c][0] * length, sum(plan[c]) * length)
+        held = {0: [tokens[rows], cotangent[rows]]}
         for bit in reversed(mp_bits[1:]):
             for k in list(held):
                 held[k | bit] = [swap(after(x, *wait), "mp", mp, bit) for x in held[k]]
@@ -751,56 +755,58 @@
 
     weights = (qkv_weight, up_weight, down_weight, out_weight)
 
-    def near_sums(keep, send):
-        other = swap(send, "mp", mp, 1)
-        column = lambda x, j: x[:, :, j * cols : (j + 1) * cols]
-        held = {2 * j: [column(keep, j), column(other, j)] for j in range(mp // 2)}
-        held[0] = [keep, other]
-        return held
-
-    def far_gives(held, bit):
-        gone = [k for k in held if k & bit]
-        return gone, jnp.concatenate([sum(x.astype(F32) for x in held[k]).astype(BF) for k in gone], 0)
-
-    def far_sums(held, first_give, wait):
-        for bit in mp_bits[1:]:
-            gone, give = first_give if bit == 2 else far_gives(held, bit)
-            moved = swap(after(give, *wait) if wait else give, "mp", mp, bit)
-            wait = (moved,)
-            for j, k in enumerate(gone):
-                held[k ^ bit].append(moved[2 * j : 2 * j + 2])
-                del held[k]
-        return held[0], wait
+    def near_sums(outs):
+        held = {k: [outs[k], [swap(x, "mp", mp, 1) for x in outs[k | 1]]] for k in reversed(range(0, mp, 2))}
+        return held, far_gives(held, mp_bits[1:2])
+
+    def far_gives(held, bits):
+        gone = [k for k in held if k & bits[0]] if bits else []
+        return {k: [sum(x[w].astype(F32) for x in held[k]).astype(BF) for w in range(2)] for k in gone}
+
+    def far_sums(held, gives, which, wait):
+        terms = {k: [x[which] for x in held[k]] for k in held}
+        moved = None
+        for i, bit in enumerate(mp_bits[1:]):
+            for k in [k for k in terms if k & bit]:
+                gone = terms.pop(k)
+                give = sum(x.astype(F32) for x in gone).astype(BF) if i else gives[k][which]
+                moved = swap(after(give, *wait), "mp", mp, bit)
+                terms[k ^ bit].append(moved)
+        return terms[0], moved
+
+    def woven(one, two):
+        return [x for pair in zip(one, two) for x in pair]
 
     acc = None
     partials, totals = [], []
     far = far_rows(0, (both,))
     for c in range(chunks):
-        scal = jnp.concatenate([lengths[c * seqs : (c + 1) * seqs], me[None]])
-        wait = () if c == 0 else (partials[-1][0],)
+        begin, seqs = plan[c]
+        scal = jnp.concatenate([lengths[begin : begin + seqs], me[None]])
+        wait = () if c == 0 else (partials[-1][0][0],)
         received = near_rows(far, wait)
         if c + 1 < chunks:
-            far = far_rows(c + 1, (received[-1], sources[-1], f_split))
-        keep, send, *acc = block_call(
-            c, seqs, c == chunks - 1, sizes, acc, scal, whole_rows, received, small, weights,
+            far = far_rows(c + 1, (received[-1],))
+        if c:
+            held, gives = near_sums(partials[-1])
+            ended = [far_sums(held, gives, w, (received[-1],)) for w in range(2)]
+            moved = [x[1] for x in ended if x[1] is not None]
+            totals.append(woven(ended[0][0], ended[1][0]))
+            scal = after(scal, *[x for give in gives.values() for x in give])
+        found = block_call(
+            begin, seqs, c == chunks - 1, sizes, acc, scal, whole_rows, received, small, weights,
             (f_split, sources), length, mp,
         )
-        partials.append((keep, send))
+        partials.append([found[2 * k : 2 * k + 2] for k in range(mp)])
+        acc = after(found[2 * mp :], *moved) if c else found[2 * mp :]
 
     split_sum, *input_sums = acc
     grads_both = reduce_inputs(input_sums, sizes, dim, dp, mp)
-    wait = (grads_both,)
-    for c in range(chunks - 1):
-        held = near_sums(*partials[c])
-        give = far_gives(held, 2)
-        split_sum = after(split_sum, give[1])
-        total, wait = far_sums(held, give, wait)
-        totals.append(total)
-    split_grad = reduce_rows(split_sum, dp)
-    own_both = reduce_rows(grads_both.astype(BF), dp)
-    own_both, split_grad = after((own_both, split_grad), *wait)
-    held = near_sums(*partials[-1])
-    last_give = far_gives(held, 2)
+    held, gives = near_sums(partials[-1])
+    split_sum = after(split_sum, *[x for give in gives.values() for x in give])
+    last_result, _ = far_sums(held, gives, 0, (grads_both,))
+    owned = reduce_rows(jnp.concatenate([grads_both.astype(BF), split_sum], 1), dp)
+    own_both, split_grad = owned[:, : grads_both.shape[1]], owned[:, grads_both.shape[1] :]
     cut = own_both.shape[1] - 2 * own_cols
     in_grad = own_both[:, :cut].reshape(own_ranks, 2, -1, rank).transpose(1, 2, 0, 3).reshape(in_factor.shape)
     res_grad = jnp.stack([own_both[:, cut : cut + own_cols], own_both[:, cut + own_cols :]])
@@ -812,17 +818,17 @@
     new_out, out_pruned = adam_step(out_factor, out_moments, out_owned)
     new_down, down_pruned = adam_step(down_factor, down_moments, down_owned)
     new_res, res_pruned = adam_step(res_factor, res_moments, res_grad)
-    both = spread_inputs(low(new_in), low(new_res), mp)
-    total, _ = far_sums(held, last_give, (both,))
-    totals.append(total)
-    split_whole = gather_rows(rank_rows(new_qkv, new_up, new_down, new_out), dp)
+    both = spread_inputs(low(new_in), low(new_res), mp, last_result[-1:])
+    last_grad, _ = far_sums(held, gives, 1, (both,))
+    totals.append(woven(last_result, last_grad))
     merged_qkv, merged_up, merged_down, merged_out = merge_call(
-        me[None], weights, split_whole, gather_inputs(both, sizes, dim, dp, mp), sizes, dp
+        me[None], weights,
+        *gather_factors(both, rank_rows(new_qkv, new_up, new_down, new_out), sizes, dim, dp, mp), sizes, dp,
     )
     ended = []
     for c in range(chunks):
         ended = finish_call(
-            c, lengths[c * seqs : (c + 1) * seqs], totals[c], tokens, cotangent, res_bias, length, ended
+            plan[c][0], lengths[plan[c][0] : sum(plan[c])], totals[c], tokens, cotangent, res_bias, length, ended
         )
     result, grad_tokens = ended
     return (

time: 365 us -> 341 us (0.934)
  starting transfers between devices: 70.8 us -> 53.5 us
  waiting for transfers between devices: 95.7 us -> 90.2 us
  local copies, waits for them, and re-layouts: 17.4 us -> 12.4 us
    all_to_all x4 -> x2, waiting for transfers between devices: 26.5 us -> 1.39 us  [gather_rows(): lax.all_to_all(jnp.broadcast_to(x[None], (dp,) + x.shape), 'dp', 0, 0, ti...]
    ppermute x21 -> x29, waiting for transfers between devices: 41.5 us -> 65.3 us  [swap(): return lax.ppermute(x, axis, [(i, i ^ bit) for i in range(size)])]
    all_to_all x4 -> x2, starting transfers between devices: 27.8 us -> 9.38 us  [gather_rows(): lax.all_to_all(jnp.broadcast_to(x[None], (dp,) + x.shape), 'dp', 0, 0, ti...]
    all_to_all x2 -> x1, waiting for transfers between devices: 27.7 us -> 23.5 us  [reduce_rows(): lax.all_to_all(x.reshape(dp, -1, x.shape[1]), 'dp', 0, 0, tiled=True)]
    ppermute x21 -> x29, starting transfers between devices: 13.8 us -> 17.1 us  [swap(): return lax.ppermute(x, axis, [(i, i ^ bit) for i in range(size)])]
    convert_element_type x2 -> x4, other arithmetic: 8.18 us -> 5.91 us  [far_gives(): sum((x[w].astype(F32) for x in held[k])).astype(BF)]
    all_to_all x2 -> x1, starting transfers between devices: 29.2 us -> 27.1 us  [reduce_rows(): lax.all_to_all(x.reshape(dp, -1, x.shape[1]), 'dp', 0, 0, tiled=True)]
  transfers between devices with their start and end apart: 27 -> 32, of which waited for: 11 -> 11; matrix products, arithmetic and copies ran while one was open for 11% -> 13% of each run, Pallas kernels for 38% -> 40%
where the time goes in v2:
time: 341 us; the launch traced here: 334 us
  Pallas kernels  141 us (41%)
  waiting for transfers between devices  90.2 us (26%)
  starting transfers between devices  53.5 us (16%)
  other arithmetic  35.9 us (11%)
  local copies, waits for them, and re-layouts  12.4 us (4%)
    pallas_call x2, Pallas kernels, block_call(): pl.pallas_call(functools.partial(block_kernel, cfg), out_shape=[*out, *su...  123 us
    ppermute x29, waiting for transfers between devices, swap(): return lax.ppermute(x, axis, [(i, i ^ bit) for i in range(size)])  65.3 us
    all_to_all x1, starting transfers between devices, reduce_rows(): lax.all_to_all(x.reshape(dp, -1, x.shape[1]), 'dp', 0, 0, tiled=True)  27.1 us
    all_to_all x1, waiting for transfers between devices, reduce_rows(): lax.all_to_all(x.reshape(dp, -1, x.shape[1]), 'dp', 0, 0, tiled=True)  23.5 us
    ppermute x29, starting transfers between devices, swap(): return lax.ppermute(x, axis, [(i, i ^ bit) for i in range(size)])  17.1 us
    another operation x14, other arithmetic, adam_step(): jnp.stack([first_moment * keep_mask, second_moment * keep_mask])  16.7 us
    pallas_call x2, Pallas kernels, finish_call(): pl.pallas_call(functools.partial(finish_kernel, (len(parts), block, lengt...  11.9 us
    all_to_all x2, starting transfers between devices, gather_rows(): lax.all_to_all(jnp.broadcast_to(x[None], (dp,) + x.shape), 'dp', 0, 0, ti...  9.38 us
  transfers between devices with their start and end apart: 32, of which 11 were waited for; matrix products, arithmetic and copies ran while one was open for 13% of the time, Pallas kernels for 40%

profile of v2, /device:TPU:0, one launch (start us, length us, event | category | flops | bytes accessed | tf_op | source)
XLA Modules:
  0.0 334.3 jit_solution(9008544627521352439)
XLA Ops:
  1.3 0.8 convert_element_type.105
  2.0 0.8 convert_element_type.106
  2.9 3.0 collective-permute-start.2
  5.9 3.0 fusion.40
  9.0 1.2 broadcast_in_dim.26
  10.2 5.8 %all-to-all-start = ((bf16[8,16,5120]{2,1,0:T(8,128)(2,1)}), bf16[8,16,5120]{2,1,0:T(8,128)(2,1)S(1)}, u32[]{:S(2)}, u32[]{:S(2)}) async-start(bf16[8,16,5120]{2,1,0:T(8,128)(2,1)} %broadcast_in_dim.26), calls=%async_computation | async-start | bytes 2621440 | tf_op jit(solution)/shard_map/all_to_all | solution.py:621
  16.0 1.0 collective-permute-start.4
  17.0 1.1 fusion.41
  18.1 1.1 collective-permute-start.3
  19.2 23.3 %collective-permute-done.4.refs_5_ = bf16[2048,256]{1,0:T(8,128)(2,1)} collective-permute-done((bf16[2048,256]{1,0:T(8,128)(2,1)}, bf16[2048,256]{1,0:T(8,128)(2,1)}, u32[]{:S(2)}, u32[]{:S(2)}) %collective-permute-start.4) | collective-permute-done | bytes 1048608 | tf_op jit(solution)/shard_map/ppermute | solution.py:582
  42.5 20.9 %collective-permute-done.3.refs_4_ = bf16[2048,256]{1,0:T(8,128)(2,1)S(1)} collective-permute-done((bf16[2048,256]{1,0:T(8,128)(2,1)S(1)}, bf16[2048,256]{1,0:T(8,128)(2,1)S(1)}, u32[]{:S(2)}, u32[]{:S(2)}) %collective-permute-start.3) | collective-permute-done | bytes 1048608 | tf_op jit(solution)/shard_map/ppermute | solution.py:582
  64.0 0.7 broadcast_in_dim.11.refs_10_
  65.9 1.5 collective-permute-start.11
  67.4 0.6 broadcast_1_refs_22__refs_23_.2.refs_22_.refs_23_
  68.2 57.0 %block.2 = (bf16[2048,256]{1,0:T(8,128)(2,1)}, bf16[2048,256]{1,0:T(8,128)(2,1)}, bf16[2048,256]{1,0:T(8,128)(2,1)}, bf16[2048,256]{1,0:T(8,128)(2,1)}, bf16[204...) custom-call(s32[3]{0:T(128)} %pad_add_fusion.1.scal, ...), custom_call_target="tpu_custom_call" | custom-call | flops 96636764160 | bytes 33554432 | tf_op jit(solution)/shard_map/block/pallas_call | solution.py:436
  126.9 1.3 collective-permute-done.8
  128.1 1.5 add_convert_fusion.3
  129.7 1.5 collective-permute-done.9
  131.1 1.3 add_convert_fusion.2
  133.6 1.1 collective-permute-start.18
  134.7 66.0 %block.3 = (bf16[2048,256]{1,0:T(8,128)(2,1)}, bf16[2048,256]{1,0:T(8,128)(2,1)}, bf16[2048,256]{1,0:T(8,128)(2,1)}, bf16[2048,256]{1,0:T(8,128)(2,1)}, bf16[204...) custom-call(s32[3]{0:T(128)} %pad_add_fusion.scal, ...), custom_call_target="tpu_custom_call" | custom-call | flops 96636764160 | bytes 33554432 | tf_op jit(solution)/shard_map/block/pallas_call | solution.py:436
  201.9 2.5 collective-permute-done.16
  204.3 2.8 add_convert_fusion.1
  207.4 1.0 collective-permute-start.21
  208.7 7.1 %collective-permute-done.21 = bf16[128,1024]{1,0:T(8,128)(2,1)S(1)} collective-permute-done((bf16[128,1024]{1,0:T(8,128)(2,1)S(1)}, bf16[128,1024]{1,0:T(8,128)(2,1)S(1)}, u32[]{:S(2)}, u32[]{:S(2)}) %collective-permute-start.21) | collective-permute-done | bytes 262176 | tf_op jit(solution)/shard_map/ppermute | solution.py:582
  215.9 1.0 pad_maximum_fusion
  216.9 27.1 %all-to-all-start.1 = ((bf16[8,16,4096]{2,1,0:T(8,128)(2,1)}), bf16[8,16,4096]{2,1,0:T(8,128)(2,1)S(1)}, u32[]{:S(2)}, u32[]{:S(2)}) async-start(bf16[8,16,4096]{2,1,0:T(8,128)(2,1)} %bitcast.15), calls=%async_computation.1 | async-start | bytes 2097152 | tf_op jit(solution)/shard_map/all_to_all | solution.py:659
  245.0 1.0 collective-permute-start.22
  246.0 23.5 %all-to-all-done.1 = bf16[8,16,4096]{2,1,0:T(8,128)(2,1)S(1)} async-done(((bf16[8,16,4096]{2,1,0:T(8,128)(2,1)}), bf16[8,16,4096]{2,1,0:T(8,128)(2,1)S(1)}, u32[]{:S(2)}, u32[]{:S(2)}) %all-to-all-start.1) | async-done | bytes 1048608 | tf_op jit(solution)/shard_map/all_to_all | solution.py:659
  270.3 0.8 fusion.33
  271.2 1.4 fusion.32
  272.6 0.6 select_bitcast_fusion.5
  273.2 1.5 select_bitcast_fusion.3
  274.7 1.5 select_bitcast_fusion.1
  276.2 1.0 collective-permute-start.27
  277.2 1.3 select_bitcast_fusion.7
  278.5 2.0 collective-permute-done.27
  280.5 1.0 collective-permute-start.24
  281.5 0.9 constant_dynamic-update-slice_fusion.21
  282.4 1.0 constant_dynamic-update-slice_fusion.20
  283.4 1.0 constant_dynamic-update-slice_fusion.19
  284.3 0.8 constant_dynamic-update-slice_fusion.18
  285.1 1.2 broadcast_in_dim.27
  286.3 3.6 %all-to-all-start.2 = ((bf16[8,16,5120]{2,1,0:T(8,128)(2,1)}), bf16[8,16,5120]{2,1,0:T(8,128)(2,1)S(1)}, u32[]{:S(2)}, u32[]{:S(2)}) async-start(bf16[8,16,5120]{2,1,0:T(8,128)(2,1)} %broadcast_in_dim.27), calls=%async_computation.2 | async-start | bytes 2621440 | tf_op jit(solution)/shard_map/all_to_all | solution.py:621
  289.9 6.0 %finish.2 = (f32[4096,256]{1,0:T(8,128)}, f32[4096,256]{1,0:T(8,128)}) custom-call(s32[2]{0:T(128)} %copy-done.27, bf16[2048,256]{1,0:T(8,128)(2,1)} %get-tuple-element.75.refs_0_, bf16[2048,256]{1,0:T(8,128)(2,1)} %get-tuple-element.100.refs_1_, bf16[2048,256]{1,0:T(8,128)(2,1)} %collective-permute-done.25.refs_2_, ...), custom_call_target="tpu_custom_call" | custom-call | flops 4194304 | bytes 10485760 | tf_op jit(solution)/shard_map/finish/pallas_call | solution.py:499
  295.9 6.7 %collective-permute-done.24.refs_5_ = bf16[2048,256]{1,0:T(8,128)(2,1)} collective-permute-done((bf16[2048,256]{1,0:T(8,128)(2,1)S(1)}, bf16[2048,256]{1,0:T(8,128)(2,1)}, u32[]{:S(2)}, u32[]{:S(2)}) %collective-permute-start.24) | collective-permute-done | bytes 1048608 | tf_op jit(solution)/shard_map/ppermute | solution.py:582
  302.6 5.9 %finish.3 = (f32[4096,256]{1,0:T(8,128)}, f32[4096,256]{1,0:T(8,128)}) custom-call(s32[2]{0:T(128)} %copy-done.26, bf16[2048,256]{1,0:T(8,128)(2,1)} %get-tuple-element.80.refs_0_, bf16[2048,256]{1,0:T(8,128)(2,1)} %get-tuple-element.81.refs_1_, bf16[2048,256]{1,0:T(8,128)(2,1)} %copy-done.8, ...), custom_call_target="tpu_custom_call", output_to_operand_aliasing={{0}: (10, {}), {1}: (11, {})} | custom-call | flops 4194304 | bytes 10485760 | tf_op jit(solution)/shard_map/finish/pallas_call | solution.py:499
  308.6 0.9 fusion.29
  309.5 0.8 fusion.25
  310.3 0.6 pad_maximum_fusion.5
  310.9 0.8 add_select_fusion
  311.7 0.8 fusion.27
  313.1 0.9 select_bitcast_fusion.4
  314.0 1.4 pad_maximum_fusion.3
  315.5 1.3 select_bitcast_fusion.6
  316.8 1.5 select_bitcast_fusion.2
  318.3 1.4 all-to-all-done.2.refs_5_
  319.8 1.4 pad_maximum_fusion.8
  321.2 1.5 pad_maximum_fusion.1
  322.7 0.9 select_bitcast_fusion
  323.6 1.5 pad_maximum_fusion.2
  325.1 1.6 copy-done.1
  326.7 1.4 copy-done.2
  328.1 6.0 %merge.1 = (f32[1024,768]{1,0:T(8,128)}, f32[1024,1024]{1,0:T(8,128)}, f32[1024,1024]{1,0:T(8,128)}, f32[256,1024]{1,0:T(8,128)}) custom-call(s32[1]{0:T(128)} %bitcast.scal, bf16[1024,768]{1,0:T(8,128)(2,1)S(1)} %copy-done.2, bf16[1024,1024]{1,0:T(8,128)(2,1)S(1)} %copy-done, bf16[1024,1024]{1,0:T(8,128)(2,1)S(1)} %copy-done.1, ...), custom_call_target="tpu_custom_call" | custom-call | flops 805306368 | bytes 20971520 | tf_op jit(solution)/shard_map/merge/pallas_call | solution.py:553
  (142 shorter events, 9.8 us)
Async XLA Ops:
  0.7 65.2 %collective-permute-start = (bf16[4096,256]{1,0:T(8,128)(2,1)}, bf16[4096,256]{1,0:T(8,128)(2,1)}, u32[]{:S(2)}, u32[]{:S(2)}) collective-permute-start(bf16[4096,256]{1,0:T(8,128)(2,1)} %refs_6_.3), channel_id=1, source_target_pairs={{0,1},{1,0},{2,3},{3,2},{4,5},{5,4},{6,7},{7,6},{8,9},{9,8},{10,11... | collective-permute-start | bytes 6291464 | tf_op jit(solution)/shard_map/ppermute | solution.py:582
  1.2 66.2 %collective-permute-start.1 = (bf16[4096,256]{1,0:T(8,128)(2,1)}, bf16[4096,256]{1,0:T(8,128)(2,1)}, u32[]{:S(2)}, u32[]{:S(2)}) collective-permute-start(bf16[4096,256]{1,0:T(8,128)(2,1)} %refs_7_.3), channel_id=1, source_target_pairs={{0,1},{1,0},{2,3},{3,2},{4,5},{5,4},{6,7},{7,6},{8,9},{9,8},{10,11... | collective-permute-start | bytes 6291464 | tf_op jit(solution)/shard_map/ppermute | solution.py:582
  2.8 6.1 %copy-start.21 = (f32[16,768]{1,0:T(8,128)S(1)}, f32[16,768]{1,0:T(8,128)}, u32[]{:S(2)}) copy-start(f32[16,768]{1,0:T(8,128)} %param.38) | copy-start | bytes 147460
  2.8 6.1 %copy-start.17 = (f32[16,1024]{1,0:T(8,128)S(1)}, f32[16,1024]{1,0:T(8,128)}, u32[]{:S(2)}) copy-start(f32[16,1024]{1,0:T(8,128)} %param.39) | copy-start | bytes 196612
  2.8 6.1 %copy-start.18 = (f32[1024,16]{0,1:T(8,128)S(1)}, f32[1024,16]{0,1:T(8,128)}, u32[]{:S(2)}) copy-start(f32[1024,16]{0,1:T(8,128)} %param.41) | copy-start | bytes 196612
  2.8 6.1 %copy-start.24 = (f32[256,16]{0,1:T(8,128)S(1)}, f32[256,16]{0,1:T(8,128)}, u32[]{:S(2)}) copy-start(f32[256,16]{0,1:T(8,128)} %param.40) | copy-start | bytes 49156
  2.9 6.0 %collective-permute-start.2 = (bf16[16,1024]{1,0:T(8,128)(2,1)S(1)}, bf16[16,1024]{1,0:T(8,128)(2,1)S(1)}, u32[]{:S(2)}, u32[]{:S(2)}) collective-permute-start(bf16[16,1024]{1,0:T(8,128)(2,1)S(1)} %constant_dynamic-update-slice_fusion), channel_id=1, source_target_pairs={{0,2},{1,3},{2,0},{3,1},{4,6},{5,7},{6,4},{7,5},{8,10},{9,11},{10,... | collective-permute-start | bytes 98312 | tf_op jit(solution)/shard_map/ppermute | solution.py:582
  9.0 8.0 %copy-start.4 = (bf16[4096,256]{1,0:T(8,128)(2,1)S(1)}, bf16[4096,256]{1,0:T(8,128)(2,1)}, u32[]{:S(2)}) copy-start(bf16[4096,256]{1,0:T(8,128)(2,1)} %refs_6_.3) | copy-start | bytes 6291460
  10.2 53.2 %all-to-all-start = ((bf16[8,16,5120]{2,1,0:T(8,128)(2,1)}), bf16[8,16,5120]{2,1,0:T(8,128)(2,1)S(1)}, u32[]{:S(2)}, u32[]{:S(2)}) async-start(bf16[8,16,5120]{2,1,0:T(8,128)(2,1)} %broadcast_in_dim.26), calls=%async_computation | async-start | bytes 2621440 | tf_op jit(solution)/shard_map/all_to_all | solution.py:621
  16.0 48.0 %copy-start.25 = (f32[768]{0:T(1024)S(1)}, f32[768]{0:T(1024)}, u32[]{:S(2)}) copy-start(f32[768]{0:T(1024)} %param.34) | copy-start | bytes 9220
  16.0 48.7 %copy-start.28 = (s32[4]{0:T(128)S(1)}, s32[4]{0:T(128)}, u32[]{:S(2)}) copy-start(s32[4]{0:T(128)} %param.27) | copy-start | bytes 52
  16.0 26.5 %collective-permute-start.4 = (bf16[2048,256]{1,0:T(8,128)(2,1)}, bf16[2048,256]{1,0:T(8,128)(2,1)}, u32[]{:S(2)}, u32[]{:S(2)}) collective-permute-start(bf16[2048,256]{1,0:T(8,128)(2,1)} %get-tuple-element.67), channel_id=1, source_target_pairs={{0,2},{1,3},{2,0},{3,1},{4,6},{5,7},{6,4},{7,5},{8,10},{9,11},{10,... | collective-permute-start | bytes 3145736 | tf_op jit(solution)/shard_map/ppermute | solution.py:582
  18.1 45.2 %collective-permute-start.3 = (bf16[2048,256]{1,0:T(8,128)(2,1)S(1)}, bf16[2048,256]{1,0:T(8,128)(2,1)S(1)}, u32[]{:S(2)}, u32[]{:S(2)}) collective-permute-start(bf16[2048,256]{1,0:T(8,128)(2,1)S(1)} %get-tuple-element.66), channel_id=1, source_target_pairs={{0,2},{1,3},{2,0},{3,1},{4,6},{5,7},{6,4},{7,5},{8,10},{9,11},{10,... | collective-permute-start | bytes 3145736 | tf_op jit(solution)/shard_map/ppermute | solution.py:582
  42.5 22.9 %collective-permute-start.6 = (bf16[2048,256]{1,0:T(8,128)(2,1)}, bf16[2048,256]{1,0:T(8,128)(2,1)S(1)}, u32[]{:S(2)}, u32[]{:S(2)}) collective-permute-start(bf16[2048,256]{1,0:T(8,128)(2,1)} %collective-permute-done.4.refs_5_), channel_id=1, source_target_pairs={{0,1},{1,0},{2,3},{3,2},{4,5},{5,4},{6,7},{7,6},{8,9},{9,8},{10,11... | collective-permute-start | bytes 3145736 | tf_op jit(solution)/shard_map/ppermute | solution.py:582
  63.3 4.7 %copy-start.29 = (bf16[2048,256]{1,0:T(8,128)(2,1)}, bf16[2048,256]{1,0:T(8,128)(2,1)S(1)}, u32[]{:S(2)}) copy-start(bf16[2048,256]{1,0:T(8,128)(2,1)S(1)} %collective-permute-done.3.refs_4_) | copy-start | bytes 3145732
  63.3 4.1 %collective-permute-start.5 = (bf16[2048,256]{1,0:T(8,128)(2,1)S(1)}, bf16[2048,256]{1,0:T(8,128)(2,1)}, u32[]{:S(2)}, u32[]{:S(2)}) collective-permute-start(bf16[2048,256]{1,0:T(8,128)(2,1)S(1)} %collective-permute-done.3.refs_4_), channel_id=1, source_target_pairs={{0,1},{1,0},{2,3},{3,2},{4,5},{5,4},{6,7},{7,6},{8,9},{9,8},{10,11... | collective-permute-start | bytes 3145736 | tf_op jit(solution)/shard_map/ppermute | solution.py:582
  63.4 4.7 %copy-start.5 = (bf16[8,16,5120]{2,1,0:T(8,128)(2,1)}, bf16[8,16,5120]{2,1,0:T(8,128)(2,1)S(1)}, u32[]{:S(2)}) copy-start(bf16[8,16,5120]{2,1,0:T(8,128)(2,1)S(1)} %all-to-all-done.refs_18_) | copy-start | bytes 3932164
  63.4 4.0 %collective-permute-start.7 = (bf16[128,2048]{1,0:T(8,128)(2,1)S(1)}, bf16[128,2048]{1,0:T(8,128)(2,1)S(1)}, u32[]{:S(2)}, u32[]{:S(2)}) collective-permute-start(bf16[128,2048]{1,0:T(8,128)(2,1)S(1)} %slice.163), channel_id=1, source_target_pairs={{0,1},{1,0},{2,3},{3,2},{4,5},{5,4},{6,7},{7,6},{8,9},{9,8},{10,11... | collective-permute-start | bytes 1572872 | tf_op jit(solution)/shard_map/ppermute | solution.py:582
  64.8 60.4 %copy-start.27 = (s32[2]{0:T(128)}, s32[2]{0:T(128)S(1)}, u32[]{:S(2)}) copy-start(s32[2]{0:T(128)S(1)} %get-tuple-element.144.lens) | copy-start | bytes 28
  64.8 61.0 %copy-start.26 = (s32[2]{0:T(128)}, s32[2]{0:T(128)S(1)}, u32[]{:S(2)}) copy-start(s32[2]{0:T(128)S(1)} %get-tuple-element.145.lens) | copy-start | bytes 28
  65.4 2.7 copy-start.30
  65.4 61.0 %collective-permute-start.10 = (bf16[2048,256]{1,0:T(8,128)(2,1)}, bf16[2048,256]{1,0:T(8,128)(2,1)}, u32[]{:S(2)}, u32[]{:S(2)}) collective-permute-start(bf16[2048,256]{1,0:T(8,128)(2,1)} %get-tuple-element.73), channel_id=1, source_target_pairs={{0,2},{1,3},{2,0},{3,1},{4,6},{5,7},{6,4},{7,5},{8,10},{9,11},{10,... | collective-permute-start | bytes 3145736 | tf_op jit(solution)/shard_map/ppermute | solution.py:582
  65.9 60.6 %collective-permute-start.11 = (bf16[2048,256]{1,0:T(8,128)(2,1)}, bf16[2048,256]{1,0:T(8,128)(2,1)}, u32[]{:S(2)}, u32[]{:S(2)}) collective-permute-start(bf16[2048,256]{1,0:T(8,128)(2,1)} %get-tuple-element.74), channel_id=1, source_target_pairs={{0,2},{1,3},{2,0},{3,1},{4,6},{5,7},{6,4},{7,5},{8,10},{9,11},{10,... | collective-permute-start | bytes 3145736 | tf_op jit(solution)/shard_map/ppermute | solution.py:582
  125.2 5.9 %copy-start.10 = (bf16[2048,256]{1,0:T(8,128)(2,1)S(1)}, bf16[2048,256]{1,0:T(8,128)(2,1)}, u32[]{:S(2)}) copy-start(bf16[2048,256]{1,0:T(8,128)(2,1)} %get-tuple-element.70) | copy-start | bytes 3145732
  125.2 2.9 collective-permute-start.8
  125.3 5.9 %collective-permute-start.9 = (bf16[2048,256]{1,0:T(8,128)(2,1)}, bf16[2048,256]{1,0:T(8,128)(2,1)S(1)}, u32[]{:S(2)}, u32[]{:S(2)}) collective-permute-start(bf16[2048,256]{1,0:T(8,128)(2,1)} %get-tuple-element.71), channel_id=1, source_target_pairs={{0,1},{1,0},{2,3},{3,2},{4,5},{5,4},{6,7},{7,6},{8,9},{9,8},{10,11... | collective-permute-start | bytes 3145736 | tf_op jit(solution)/shard_map/ppermute | solution.py:582
  126.4 8.3 %collective-permute-start.12 = (bf16[2048,256]{1,0:T(8,128)(2,1)}, bf16[2048,256]{1,0:T(8,128)(2,1)}, u32[]{:S(2)}, u32[]{:S(2)}) collective-permute-start(bf16[2048,256]{1,0:T(8,128)(2,1)} %collective-permute-done.10.refs_4_), channel_id=1, source_target_pairs={{0,1},{1,0},{2,3},{3,2},{4,5},{5,4},{6,7},{7,6},{8,9},{9,8},{10,11... | collective-permute-start | bytes 3145736 | tf_op jit(solution)/shard_map/ppermute | solution.py:582
  126.4 6.2 %collective-permute-start.13 = (bf16[2048,256]{1,0:T(8,128)(2,1)}, bf16[2048,256]{1,0:T(8,128)(2,1)S(1)}, u32[]{:S(2)}, u32[]{:S(2)}) collective-permute-start(bf16[2048,256]{1,0:T(8,128)(2,1)} %collective-permute-done.11.refs_5_), channel_id=1, source_target_pairs={{0,1},{1,0},{2,3},{3,2},{4,5},{5,4},{6,7},{7,6},{8,9},{9,8},{10,11... | collective-permute-start | bytes 3145736 | tf_op jit(solution)/shard_map/ppermute | solution.py:582
  132.6 1.0 copy-start.31
  132.6 68.7 %collective-permute-start.17 = (bf16[2048,256]{1,0:T(8,128)(2,1)S(1)}, bf16[2048,256]{1,0:T(8,128)(2,1)S(1)}, u32[]{:S(2)}, u32[]{:S(2)}) collective-permute-start(bf16[2048,256]{1,0:T(8,128)(2,1)S(1)} %add_convert_fusion.3), channel_id=1, source_target_pairs={{0,2},{1,3},{2,0},{3,1},{4,6},{5,7},{6,4},{7,5},{8,10},{9,11},{10,... | collective-permute-start | bytes 3145736 | tf_op jit(solution)/shard_map/ppermute | solution.py:582
  133.6 67.7 %collective-permute-start.18 = (bf16[2048,256]{1,0:T(8,128)(2,1)}, bf16[2048,256]{1,0:T(8,128)(2,1)S(1)}, u32[]{:S(2)}, u32[]{:S(2)}) collective-permute-start(bf16[2048,256]{1,0:T(8,128)(2,1)} %add_convert_fusion.2), channel_id=1, source_target_pairs={{0,2},{1,3},{2,0},{3,1},{4,6},{5,7},{6,4},{7,5},{8,10},{9,11},{10,... | collective-permute-start | bytes 3145736 | tf_op jit(solution)/shard_map/ppermute | solution.py:582
  200.7 6.5 %copy-start.20 = (bf16[2,8,16,512]{3,2,1,0:T(8,128)(2,1)S(1)}, bf16[2,8,16,512]{3,2,1,0:T(8,128)(2,1)}, u32[]{:S(2)}) copy-start(bf16[2,8,16,512]{3,2,1,0:T(8,128)(2,1)} %get-tuple-element.93) | copy-start | bytes 786436
  200.7 3.6 %collective-permute-start.16 = (bf16[2048,256]{1,0:T(8,128)(2,1)}, bf16[2048,256]{1,0:T(8,128)(2,1)}, u32[]{:S(2)}, u32[]{:S(2)}) collective-permute-start(bf16[2048,256]{1,0:T(8,128)(2,1)} %get-tuple-element.85), channel_id=1, source_target_pairs={{0,1},{1,0},{2,3},{3,2},{4,5},{5,4},{6,7},{7,6},{8,9},{9,8},{10,11... | collective-permute-start | bytes 3145736 | tf_op jit(solution)/shard_map/ppermute | solution.py:582
  200.8 7.6 %collective-permute-start.23 = (bf16[2048,256]{1,0:T(8,128)(2,1)}, bf16[2048,256]{1,0:T(8,128)(2,1)S(1)}, u32[]{:S(2)}, u32[]{:S(2)}) collective-permute-start(bf16[2048,256]{1,0:T(8,128)(2,1)} %get-tuple-element.99), channel_id=1, source_target_pairs={{0,1},{1,0},{2,3},{3,2},{4,5},{5,4},{6,7},{7,6},{8,9},{9,8},{10,11... | collective-permute-start | bytes 3145736 | tf_op jit(solution)/shard_map/ppermute | solution.py:582
  201.3 6.0 %copy-start.6 = (bf16[2048,256]{1,0:T(8,128)(2,1)}, bf16[2048,256]{1,0:T(8,128)(2,1)S(1)}, u32[]{:S(2)}) copy-start(bf16[2048,256]{1,0:T(8,128)(2,1)S(1)} %collective-permute-done.17.refs_4_) | copy-start | bytes 3145732
  201.3 6.0 %copy-start.7 = (bf16[2048,256]{1,0:T(8,128)(2,1)}, bf16[2048,256]{1,0:T(8,128)(2,1)S(1)}, u32[]{:S(2)}) copy-start(bf16[2048,256]{1,0:T(8,128)(2,1)S(1)} %collective-permute-done.18.refs_5_) | copy-start | bytes 3145732
  201.3 5.9 %collective-permute-start.19 = (bf16[2,8,16,512]{3,2,1,0:T(8,128)(2,1)}, bf16[2,8,16,512]{3,2,1,0:T(8,128)(2,1)S(1)}, u32[]{:S(2)}, u32[]{:S(2)}) collective-permute-start(bf16[2,8,16,512]{3,2,1,0:T(8,128)(2,1)} %get-tuple-element.94), channel_id=1, source_target_pairs={{0,1},{1,0},{2,3},{3,2},{4,5},{5,4},{6,7},{7,6},{8,9},{9,8},{10,11... | collective-permute-start | bytes 786440 | tf_op jit(solution)/shard_map/ppermute | solution.py:582
  201.5 5.8 %collective-permute-start.20 = (bf16[2,128,512]{2,1,0:T(8,128)(2,1)}, bf16[2,128,512]{2,1,0:T(8,128)(2,1)S(1)}, u32[]{:S(2)}, u32[]{:S(2)}) collective-permute-start(bf16[2,128,512]{2,1,0:T(8,128)(2,1)} %get-tuple-element.96), channel_id=1, source_target_pairs={{0,1},{1,0},{2,3},{3,2},{4,5},{5,4},{6,7},{7,6},{8,9},{9,8},{10,11... | collective-permute-start | bytes 786440 | tf_op jit(solution)/shard_map/ppermute | solution.py:582
  204.3 2.9 copy-start.19
  207.2 1.3 copy-start.9
  207.4 8.4 %collective-permute-start.21 = (bf16[128,1024]{1,0:T(8,128)(2,1)S(1)}, bf16[128,1024]{1,0:T(8,128)(2,1)S(1)}, u32[]{:S(2)}, u32[]{:S(2)}) collective-permute-start(bf16[128,1024]{1,0:T(8,128)(2,1)S(1)} %fusion.5), channel_id=1, source_target_pairs={{0,2},{1,3},{2,0},{3,1},{4,6},{5,7},{6,4},{7,5},{8,10},{9,11},{10,... | collective-permute-start | bytes 786440 | tf_op jit(solution)/shard_map/ppermute | solution.py:582
  208.4 7.4 %copy-start.11 = (bf16[128,3072]{1,0:T(8,128)(2,1)S(1)}, bf16[128,3072]{1,0:T(8,128)(2,1)}, u32[]{:S(2)}) copy-start(bf16[128,3072]{1,0:T(8,128)(2,1)} %get-tuple-element.108) | copy-start | bytes 2359300
  216.9 53.3 %copy-start.23 = (f32[2,32,128]{2,1,0:T(8,128)S(1)}, f32[2,32,128]{2,1,0:T(8,128)}, u32[]{:S(2)}) copy-start(f32[2,32,128]{2,1,0:T(8,128)} %param.37) | copy-start | bytes 98308
  216.9 55.6 %copy-start.16 = (f32[2,16,768]{2,1,0:T(8,128)S(1)}, f32[2,16,768]{2,1,0:T(8,128)}, u32[]{:S(2)}) copy-start(f32[2,16,768]{2,1,0:T(8,128)} %param.44) | copy-start | bytes 294916
  216.9 52.5 %all-to-all-start.1 = ((bf16[8,16,4096]{2,1,0:T(8,128)(2,1)}), bf16[8,16,4096]{2,1,0:T(8,128)(2,1)S(1)}, u32[]{:S(2)}, u32[]{:S(2)}) async-start(bf16[8,16,4096]{2,1,0:T(8,128)(2,1)} %bitcast.15), calls=%async_computation.1 | async-start | bytes 2097152 | tf_op jit(solution)/shard_map/all_to_all | solution.py:659
  244.0 45.9 %collective-permute-start.25 = (bf16[2048,256]{1,0:T(8,128)(2,1)}, bf16[2048,256]{1,0:T(8,128)(2,1)}, u32[]{:S(2)}, u32[]{:S(2)}) collective-permute-start(bf16[2048,256]{1,0:T(8,128)(2,1)} %get-tuple-element.101), channel_id=1, source_target_pairs={{0,1},{1,0},{2,3},{3,2},{4,5},{5,4},{6,7},{7,6},{8,9},{9,8},{10,11... | collective-permute-start | bytes 3145736 | tf_op jit(solution)/shard_map/ppermute | solution.py:582
  244.0 45.9 %collective-permute-start.26 = (bf16[2048,256]{1,0:T(8,128)(2,1)}, bf16[2048,256]{1,0:T(8,128)(2,1)}, u32[]{:S(2)}, u32[]{:S(2)}) collective-permute-start(bf16[2048,256]{1,0:T(8,128)(2,1)} %get-tuple-element.102), channel_id=1, source_target_pairs={{0,1},{1,0},{2,3},{3,2},{4,5},{5,4},{6,7},{7,6},{8,9},{9,8},{10,11... | collective-permute-start | bytes 3145736 | tf_op jit(solution)/shard_map/ppermute | solution.py:582
  244.5 51.4 %collective-permute-start.14 = (bf16[2048,256]{1,0:T(8,128)(2,1)}, bf16[2048,256]{1,0:T(8,128)(2,1)S(1)}, u32[]{:S(2)}, u32[]{:S(2)}) collective-permute-start(bf16[2048,256]{1,0:T(8,128)(2,1)} %get-tuple-element.82), channel_id=1, source_target_pairs={{0,1},{1,0},{2,3},{3,2},{4,5},{5,4},{6,7},{7,6},{8,9},{9,8},{10,11... | collective-permute-start | bytes 3145736 | tf_op jit(solution)/shard_map/ppermute | solution.py:582
  244.6 51.3 %collective-permute-start.15 = (bf16[2048,256]{1,0:T(8,128)(2,1)}, bf16[2048,256]{1,0:T(8,128)(2,1)}, u32[]{:S(2)}, u32[]{:S(2)}) collective-permute-start(bf16[2048,256]{1,0:T(8,128)(2,1)} %get-tuple-element.83), channel_id=1, source_target_pairs={{0,1},{1,0},{2,3},{3,2},{4,5},{5,4},{6,7},{7,6},{8,9},{9,8},{10,11... | collective-permute-start | bytes 3145736 | tf_op jit(solution)/shard_map/ppermute | solution.py:582
  245.0 31.2 %collective-permute-start.22 = (bf16[2048,256]{1,0:T(8,128)(2,1)}, bf16[2048,256]{1,0:T(8,128)(2,1)}, u32[]{:S(2)}, u32[]{:S(2)}) collective-permute-start(bf16[2048,256]{1,0:T(8,128)(2,1)} %add_convert_fusion.1), channel_id=1, source_target_pairs={{0,2},{1,3},{2,0},{3,1},{4,6},{5,7},{6,4},{7,5},{8,10},{9,11},{10,... | collective-permute-start | bytes 3145736 | tf_op jit(solution)/shard_map/ppermute | solution.py:582
  270.3 11.2 %copy-start.14 = (f32[16,2,2,128]{3,0,2,1:T(8,128)}, f32[16,2,2,128]{3,0,2,1:T(8,128)S(1)}, u32[]{:S(2)}) copy-start(f32[16,2,2,128]{3,0,2,1:T(8,128)S(1)} %copy.45) | copy-start | bytes 98308
  273.2 13.1 %copy-start.15 = (f32[16,768]{1,0:T(8,128)}, f32[16,768]{1,0:T(8,128)S(1)}, u32[]{:S(2)}) copy-start(f32[16,768]{1,0:T(8,128)S(1)} %get-tuple-element.127) | copy-start | bytes 147460
  274.7 42.1 %copy-start.12 = (f32[16,1024]{1,0:T(8,128)}, f32[16,1024]{1,0:T(8,128)S(1)}, u32[]{:S(2)}) copy-start(f32[16,1024]{1,0:T(8,128)S(1)} %get-tuple-element.124) | copy-start | bytes 196612
  276.2 46.5 %copy-start.13 = (f32[1024,16]{0,1:T(8,128)}, f32[1024,16]{0,1:T(8,128)S(1)}, u32[]{:S(2)}) copy-start(f32[1024,16]{0,1:T(8,128)S(1)} %get-tuple-element.118) | copy-start | bytes 196612
  276.2 4.3 %collective-permute-start.27 = (bf16[16,1024]{1,0:T(8,128)(2,1)S(1)}, bf16[16,1024]{1,0:T(8,128)(2,1)S(1)}, u32[]{:S(2)}, u32[]{:S(2)}) collective-permute-start(bf16[16,1024]{1,0:T(8,128)(2,1)S(1)} %constant_dynamic-update-slice_fusion.12), channel_id=1, source_target_pairs={{0,2},{1,3},{2,0},{3,1},{4,6},{5,7},{6,4},{7,5},{8,10},{9,11},{10,... | collective-permute-start | bytes 98312 | tf_op jit(solution)/shard_map/ppermute | solution.py:582
  278.5 36.9 %copy-start.22 = (f32[256,16]{0,1:T(8,128)}, f32[256,16]{0,1:T(8,128)S(1)}, u32[]{:S(2)}) copy-start(f32[256,16]{0,1:T(8,128)S(1)} %get-tuple-element.121) | copy-start | bytes 49156
  280.5 22.1 %collective-permute-start.24 = (bf16[2048,256]{1,0:T(8,128)(2,1)S(1)}, bf16[2048,256]{1,0:T(8,128)(2,1)}, u32[]{:S(2)}, u32[]{:S(2)}) collective-permute-start(bf16[2048,256]{1,0:T(8,128)(2,1)S(1)} %add_convert_fusion), channel_id=1, source_target_pairs={{0,2},{1,3},{2,0},{3,1},{4,6},{5,7},{6,4},{7,5},{8,10},{9,11},{10,... | collective-permute-start | bytes 3145736 | tf_op jit(solution)/shard_map/ppermute | solution.py:582
  286.3 33.4 %all-to-all-start.2 = ((bf16[8,16,5120]{2,1,0:T(8,128)(2,1)}), bf16[8,16,5120]{2,1,0:T(8,128)(2,1)S(1)}, u32[]{:S(2)}, u32[]{:S(2)}) async-start(bf16[8,16,5120]{2,1,0:T(8,128)(2,1)} %broadcast_in_dim.27), calls=%async_computation.2 | async-start | bytes 2621440 | tf_op jit(solution)/shard_map/all_to_all | solution.py:621
  295.9 6.7 %copy-start.8 = (bf16[2048,256]{1,0:T(8,128)(2,1)}, bf16[2048,256]{1,0:T(8,128)(2,1)S(1)}, u32[]{:S(2)}) copy-start(bf16[2048,256]{1,0:T(8,128)(2,1)S(1)} %collective-permute-done.14.refs_2_) | copy-start | bytes 3145732
  308.5 16.6 %copy-start = (bf16[1024,1024]{1,0:T(8,128)(2,1)S(1)}, bf16[1024,1024]{1,0:T(8,128)(2,1)}, u32[]{:S(2)}) copy-start(bf16[1024,1024]{1,0:T(8,128)(2,1)} %refs_1_.5) | copy-start | bytes 6291460
  319.7 5.4 %copy-start.3 = (bf16[256,1024]{1,0:T(8,128)(2,1)S(1)}, bf16[256,1024]{1,0:T(8,128)(2,1)}, u32[]{:S(2)}) copy-start(bf16[256,1024]{1,0:T(8,128)(2,1)} %refs_3_.1) | copy-start | bytes 1572868
  319.7 5.4 %collective-permute-start.28 = (bf16[128,2048]{1,0:T(8,128)(2,1)S(1)}, bf16[128,2048]{1,0:T(8,128)(2,1)S(1)}, u32[]{:S(2)}, u32[]{:S(2)}) collective-permute-start(bf16[128,2048]{1,0:T(8,128)(2,1)S(1)} %slice.173), channel_id=1, source_target_pairs={{0,1},{1,0},{2,3},{3,2},{4,5},{5,4},{6,7},{7,6},{8,9},{9,8},{10,11... | collective-permute-start | bytes 1572872 | tf_op jit(solution)/shard_map/ppermute | solution.py:582
  325.1 1.6 copy-start.1
  326.7 1.4 copy-start.2
  (1 other events, 0.8 us)
